TPU v7x, 32 devices: a whole 2x2x4 slice. The times are simulated.
32 devices in a mesh: ctx: 8 (over y, x, core), tp: 4 (over z).
Axes of the slice: x: 2, y: 2, z: 4, core: 2. Of those that a mesh axis runs over, the one named last changes fastest.
Arguments:
- attention: bfloat16 [4096, 2048], P('ctx', 'tp'), may hold values from -6 to 6
- residual: bfloat16 [4096, 2048], P(('ctx', 'tp')), may hold values from -6 to 6
- w_out: bfloat16 [2048, 2048], P('tp'), may hold values from -0.125 to 0.125
- w_qkv: bfloat16 [3072, 2048], P('tp'), may hold values from -0.125 to 0.125
- norm_moe: float32 [2048], replicated, may hold values from 0.25 to 1.75
- norm_attn: float32 [2048], replicated, may hold values from 0.25 to 1.75
- expert_ids: int32 [4096, 4], P(('ctx', 'tp')), may hold values from 0 to 15, all different within a row; in each aligned block of 128 rows (0 to 127, 128 to 255, ...) at most 48 rows name the same one
- expert_gates: float32 [4096, 4], P(('ctx', 'tp')), may hold values from 0.02 to 0.3
- w_gate: bfloat16 [32, 2048, 384], P(('ctx', 'tp')), may hold values from -0.125 to 0.125
- w_up: bfloat16 [32, 2048, 384], P(('ctx', 'tp')), may hold values from -0.125 to 0.125
- w_down: bfloat16 [32, 384, 2048], P(('ctx', 'tp')), may hold values from -0.21875 to 0.21875
- d_projected: bfloat16 [4096, 3072], P('ctx', 'tp'), may hold values from -6 to 6
- d_stream: bfloat16 [4096, 2048], P(('ctx', 'tp')), may hold values from -6 to 6
Outputs:
- projected: bfloat16 [4096, 3072], P('ctx', 'tp')
- stream: bfloat16 [4096, 2048], P(('ctx', 'tp'))
- grad_attention: bfloat16 [4096, 2048], P('ctx', 'tp')
- grad_residual: bfloat16 [4096, 2048], P(('ctx', 'tp'))
- grad_w_out: bfloat16 [2048, 2048], P('tp', 'ctx')
- grad_w_gate: bfloat16 [32, 2048, 384], P(('ctx', 'tp'))
- grad_w_up: bfloat16 [32, 2048, 384], P(('ctx', 'tp'))
- grad_w_down: bfloat16 [32, 384, 2048], P(('ctx', 'tp'))
Inputs may be any that keep to these rules, and one draw needn't show every extreme that they name: `expert_ids`: each row names 4 different experts. Among the rows of one device no expert is named more than 48 times, a bound that some block reaches there.
All inputs are finite; a program needn't handle non-finite values.
Results may differ from a plain program's by a relative error of at most 0.0075.
Values may be sent and summed in bfloat16 or wider, within the bound.
A program may use at most 128 MiB of HBM per device.

v0:
```python
import jax
import jax.numpy as jnp
from jax import lax
from jax.sharding import PartitionSpec as P

EPSILON = 1e-06


def swapped(block, axis, bit):
    count = lax.axis_size(axis)
    route = []
    for low in range(count):
        high = low | 1 << bit
        if high != low and high < count:
            route += [(low, high), (high, low)]
    return lax.ppermute(block, axis, route)


def rms_inverse(hidden):
    return lax.rsqrt(jnp.mean(hidden * hidden, axis=-1, keepdims=True) + EPSILON)


def rms_grad(hidden, gain_vec, inv_rms, grad_out):
    normed = hidden * inv_rms
    grad_normed = grad_out * gain_vec
    return inv_rms * (grad_normed - normed * jnp.mean(grad_normed * normed, axis=-1, keepdims=True))


def expert_inner(slot_rows, gate_mat, up_mat):
    pre_gate = jnp.dot(slot_rows, gate_mat, preferred_element_type=jnp.float32)
    pre_up = jnp.dot(slot_rows, up_mat, preferred_element_type=jnp.float32)
    active = (jax.nn.silu(pre_gate) * pre_up).astype(jnp.bfloat16)
    return (pre_gate, pre_up, active)


def half_backward(slot_rows, slot_grads, pre_gate, pre_up, active, gate_mat, up_mat, down_mat):
    sigmoid_gate = jax.nn.sigmoid(pre_gate)
    silu_gate = pre_gate * sigmoid_gate
    grad_active = jnp.einsum("sd,fd->sf", slot_grads, down_mat, preferred_element_type=jnp.float32)
    grad_gate = (
        grad_active * pre_up * sigmoid_gate * (1.0 + pre_gate * (1.0 - sigmoid_gate))
    ).astype(jnp.bfloat16)
    grad_up = (grad_active * silu_gate).astype(jnp.bfloat16)
    input_part = jnp.einsum("sf,df->sd", grad_gate, gate_mat, preferred_element_type=jnp.float32)
    input_part = (
        input_part + jnp.einsum("sf,df->sd", grad_up, up_mat, preferred_element_type=jnp.float32)
    ).astype(jnp.bfloat16)
    gate_term = jnp.einsum("sd,sf->df", slot_rows, grad_gate, preferred_element_type=jnp.float32)
    up_term = jnp.einsum("sd,sf->df", slot_rows, grad_up, preferred_element_type=jnp.float32)
    down_term = jnp.einsum("sf,sd->fd", active, slot_grads, preferred_element_type=jnp.float32)
    return (input_part, gate_term, up_term, down_term)


def tensor_rows(source, weights):
    return lax.psum_scatter(
        jnp.dot(source, weights, preferred_element_type=jnp.float32),
        "tp",
        scatter_dimension=0,
        tiled=True,
    )


def group_rows(local_rows):
    return lax.all_gather(local_rows, "tp", axis=0, tiled=True)


def dispatch_rows(payload):
    return lax.all_to_all(payload, ("ctx", "tp"), split_axis=0, concat_axis=0, tiled=True)


def return_rows(payload):
    return lax.all_to_all(payload, ("ctx", "tp"), split_axis=0, concat_axis=0, tiled=True)


def local(
    attention,
    residual,
    w_out,
    w_qkv,
    norm_moe,
    norm_attn,
    expert_ids,
    expert_gates,
    w_gate,
    w_up,
    w_down,
    d_projected,
    d_stream,
):
    ctx_count = lax.axis_size("ctx")
    tensor_count = lax.axis_size("tp")
    local_tokens = attention.shape[0] // tensor_count
    model_width = residual.shape[1]
    device_count = ctx_count * tensor_count
    expert_count = device_count // 2
    top_count = expert_ids.shape[1]
    capacity = 2 * max(1, local_tokens * top_count * 3 // (4 * expert_count))
    half_cap = capacity // 2
    slot_count = device_count * half_cap
    hidden = residual.astype(jnp.float32) + tensor_rows(attention, w_out)
    inv_one = rms_inverse(hidden)
    moe_input = (hidden * inv_one * norm_moe).astype(jnp.bfloat16)
    flat_ids = expert_ids.reshape(-1)
    expert_range = jnp.arange(expert_count, dtype=jnp.int32)
    onehot = (flat_ids[:, None] == expert_range[None, :]).astype(jnp.int32)
    position = jnp.sum((jnp.cumsum(onehot, axis=0) - onehot) * onehot, axis=1)
    slot_index = flat_ids * capacity + position
    slot_range = jnp.arange(expert_count * capacity, dtype=jnp.int32)
    matches = slot_index.reshape(local_tokens, top_count)[None, :, :] == slot_range[:, None, None]
    select = jnp.any(matches, axis=2).astype(jnp.bfloat16)
    gate_map = jnp.sum(jnp.where(matches, expert_gates[None, :, :], 0.0), axis=2)
    send_rows = jnp.dot(select, moe_input, preferred_element_type=jnp.float32).astype(jnp.bfloat16)
    arrived = dispatch_rows(send_rows.reshape(device_count, half_cap, model_width)).reshape(
        slot_count, model_width
    )
    gate_mine = w_gate[0]
    up_mine = w_up[0]
    down_mine = w_down[0]
    packed = jnp.stack([gate_mine, up_mine, down_mine.reshape(gate_mine.shape)])
    partner = swapped(packed, "tp", 0)
    gate_other = partner[0]
    up_other = partner[1]
    down_other = partner[2].reshape(down_mine.shape)
    pre_gate_one, pre_up_one, active_one = expert_inner(arrived, gate_mine, up_mine)
    pre_gate_two, pre_up_two, active_two = expert_inner(arrived, gate_other, up_other)
    out_one = jnp.dot(active_one, down_mine, preferred_element_type=jnp.float32).astype(
        jnp.bfloat16
    )
    out_two = jnp.dot(active_two, down_other, preferred_element_type=jnp.float32).astype(
        jnp.bfloat16
    )
    produced = (out_one.astype(jnp.float32) + out_two.astype(jnp.float32)).astype(jnp.bfloat16)
    returned = return_rows(produced.reshape(device_count, half_cap, model_width)).reshape(
        expert_count * capacity, model_width
    )
    picked = returned[slot_index].reshape(local_tokens, top_count, model_width)
    moe_out = jnp.sum(picked.astype(jnp.float32) * expert_gates[:, :, None], axis=1)
    stream_sum = hidden + moe_out
    stream = stream_sum.astype(jnp.bfloat16)
    inv_two = rms_inverse(stream_sum)
    attn_input = (stream_sum * inv_two * norm_attn).astype(jnp.bfloat16)
    attn_rows = group_rows(attn_input)
    projected = jnp.einsum(
        "td,od->to", attn_rows, w_qkv, preferred_element_type=jnp.float32
    ).astype(jnp.bfloat16)
    grad_attn_in = tensor_rows(d_projected, w_qkv)
    grad_stream = d_stream.astype(jnp.float32) + rms_grad(
        stream_sum, norm_attn, inv_two, grad_attn_in
    )
    grad_slots = jnp.dot(
        gate_map, grad_stream, precision=lax.Precision.HIGHEST, preferred_element_type=jnp.float32
    )
    grad_slots = grad_slots.astype(jnp.bfloat16).reshape(device_count, half_cap, model_width)
    grad_arrived = dispatch_rows(grad_slots).reshape(slot_count, model_width)
    part_one, gate_one, up_one, down_one = half_backward(
        arrived, grad_arrived, pre_gate_one, pre_up_one, active_one, gate_mine, up_mine, down_mine
    )
    part_two, gate_two, up_two, down_two = half_backward(
        arrived,
        grad_arrived,
        pre_gate_two,
        pre_up_two,
        active_two,
        gate_other,
        up_other,
        down_other,
    )
    grad_input = (part_one.astype(jnp.float32) + part_two.astype(jnp.float32)).astype(jnp.bfloat16)
    outgoing = jnp.stack([gate_two, up_two, down_two.reshape(gate_two.shape)])
    incoming = swapped(outgoing.astype(jnp.bfloat16), "tp", 0).astype(outgoing.dtype)
    gate_grad = gate_one + incoming[0]
    up_grad = up_one + incoming[1]
    down_grad = down_one + incoming[2].reshape(down_one.shape)
    back_rows = return_rows(grad_input.reshape(device_count, half_cap, model_width)).reshape(
        expert_count * capacity, model_width
    )
    grad_moe_in = jnp.sum(
        back_rows[slot_index].reshape(local_tokens, top_count, model_width).astype(jnp.float32),
        axis=1,
    )
    grad_hidden = grad_stream + rms_grad(hidden, norm_moe, inv_one, grad_moe_in)
    grad_residual = grad_hidden.astype(jnp.bfloat16)
    grad_rows_all = group_rows(grad_residual)
    grad_attention = jnp.einsum(
        "td,kd->tk", grad_rows_all, w_out, preferred_element_type=jnp.float32
    ).astype(jnp.bfloat16)
    out_partial = jnp.einsum(
        "tk,td->kd", attention, grad_rows_all, preferred_element_type=jnp.float32
    )
    out_weight_grad = lax.psum_scatter(out_partial, "ctx", scatter_dimension=1, tiled=True)
    return (
        projected,
        stream,
        grad_attention,
        grad_residual,
        out_weight_grad.astype(jnp.bfloat16),
        gate_grad.astype(jnp.bfloat16)[None],
        up_grad.astype(jnp.bfloat16)[None],
        down_grad.astype(jnp.bfloat16)[None],
    )


def solution(mesh):
    in_specs = (
        P("ctx", "tp"),
        P(("ctx", "tp"), None),
        P("tp", None),
        P("tp", None),
        P(),
        P(),
        P(("ctx", "tp"), None),
        P(("ctx", "tp"), None),
        P(("ctx", "tp"), None, None),
        P(("ctx", "tp"), None, None),
        P(("ctx", "tp"), None, None),
        P("ctx", "tp"),
        P(("ctx", "tp"), None),
    )
    out_specs = (
        P("ctx", "tp"),
        P(("ctx", "tp"), None),
        P("ctx", "tp"),
        P(("ctx", "tp"), None),
        P("tp", "ctx"),
        P(("ctx", "tp"), None, None),
        P(("ctx", "tp"), None, None),
        P(("ctx", "tp"), None, None),
    )
    return jax.shard_map(local, mesh=mesh, in_specs=in_specs, out_specs=out_specs, check_vma=False)
```

profile of v0, /device:TPU:0, one launch (start us, length us, event | category | flops | bytes accessed | tf_op | source)
XLA Modules:
  0.0 863.9 jit_solution(13506365363762189943)
XLA Ops:
  7.2 5.1 fusion.35
  15.3 76.7 %reduce-scatter.4.cloned.1.call-done = f32[128,2048]{1,0:T(8,128)} async-done(((f32[512,2048]{1,0:T(8,128)}), f32[128,2048]{1,0:T(8,128)}) %reduce-scatter.4.cloned.1.call-update) | async-done | bytes 1048592 | tf_op jit(solution)/shard_map/reduce_scatter | solution.py:55
  97.4 5.2 all-to-all-start
  107.1 5.2 pad_maximum_fusion
  117.9 207.8 %collective-permute-done = bf16[3,2048,384]{2,1,0:T(8,128)(2,1)} collective-permute-done((bf16[3,2048,384]{2,1,0:T(8,128)(2,1)}, bf16[3,2048,384]{2,1,0:T(8,128)(2,1)}, u32[]{:S(2)}, u32[]{:S(2)}) %collective-permute-start) | collective-permute-done | bytes 4718624 | tf_op jit(solution)/shard_map/ppermute | solution.py:16
  336.9 5.2 multiply_convert_fusion.5
  348.1 5.6 multiply_convert_fusion.4
  363.0 68.1 %all-to-all-done.1 = bf16[32,24,2048]{2,1,0:T(8,128)(2,1)} async-done(((bf16[32,24,2048]{2,1,0:T(8,128)(2,1)}), bf16[32,24,2048]{2,1,0:T(8,128)(2,1)}, u32[]{:S(2)}, u32[]{:S(2)}) %all-to-all-start.1) | async-done | bytes 3145760 | tf_op jit(solution)/shard_map/all_to_all | solution.py:72
  431.1 7.5 gather_fusion
  438.6 4.8 reshape.135
  443.5 5.5 multiply_reduce_fusion
  453.9 7.0 convolution_convert_fusion
  460.9 75.1 %all_to_all.20 = bf16[32,24,2048]{2,1,0:T(8,128)(2,1)S(1)} all-to-all(bf16[32,24,2048]{2,1,0:T(8,128)(2,1)S(1)} %bitcast.129), channel_id=1, replica_groups=mesh['ctx'=8,'tp'=4] {'ctx','tp'}, dimensions={0} | all-to-all | bytes 6291456 | tf_op jit(solution)/shard_map/all_to_all | solution.py:68
  551.3 74.5 %all_to_all.21 = bf16[32,24,2048]{2,1,0:T(8,128)(2,1)} all-to-all(bf16[32,24,2048]{2,1,0:T(8,128)(2,1)S(1)} %bitcast.130), channel_id=1, replica_groups=mesh['ctx'=8,'tp'=4] {'ctx','tp'}, dimensions={0} | all-to-all | bytes 6291456 | tf_op jit(solution)/shard_map/all_to_all | solution.py:72
  625.8 7.6 gather_fusion.1
  633.3 4.7 reshape.136
  638.1 5.8 reduce_sum.84
  650.4 4.6 convolution_convert_fusion.4
  672.7 38.4 %all-gather.5.cloned.1.call-done = bf16[512,2048]{1,0:T(8,128)(2,1)} async-done(((bf16[128,2048]{1,0:T(8,128)(2,1)}), bf16[512,2048]{1,0:T(8,128)(2,1)}) %all-gather.5.cloned.1.call-update) | async-done | bytes 2097168 | tf_op jit(solution)/shard_map/all_gather | solution.py:64
  711.1 5.0 convolution_bitcast_fusion
  716.2 5.2 fusion.38
  721.4 5.4 fusion.37
  726.8 101.8 %collective-permute-done.1 = bf16[3,2048,384]{2,1,0:T(8,128)(2,1)} collective-permute-done((bf16[3,2048,384]{2,1,0:T(8,128)(2,1)}, bf16[3,2048,384]{2,1,0:T(8,128)(2,1)}, u32[]{:S(2)}, u32[]{:S(2)}) %collective-permute-start.1) | collective-permute-done | bytes 4718624 | tf_op jit(solution)/shard_map/ppermute | solution.py:16
  840.0 5.9 fusion.8
  (176 shorter events, 111.3 us)
Async XLA Ops:
  7.2 106.8 %copy-start = (bf16[768,2048]{1,0:T(8,128)(2,1)S(1)}, bf16[768,2048]{1,0:T(8,128)(2,1)}, u32[]{:S(2)}) copy-start(bf16[768,2048]{1,0:T(8,128)(2,1)} %param.16) | copy-start | bytes 9437188
  7.2 84.8 %reduce-scatter.4.cloned.1.call-start = ((), (), s32[]{:S(2)}) async-start(), calls=%async_computation.7 | async-start | bytes 5242880 | tf_op jit(solution)/shard_map/reduce_scatter | solution.py:55
  13.0 80.6 %copy-start.32 = (f32[2048]{0:T(1024)S(1)}, f32[2048]{0:T(1024)}, u32[]{:S(2)}) copy-start(f32[2048]{0:T(1024)} %param.17) | copy-start | bytes 24580
  97.4 235.2 %all-to-all-start = ((bf16[32,24,2048]{2,1,0:T(8,128)(2,1)}), bf16[32,24,2048]{2,1,0:T(8,128)(2,1)}, u32[]{:S(2)}, u32[]{:S(2)}) async-start(bf16[32,24,2048]{2,1,0:T(8,128)(2,1)} %bitcast.131), calls=%async_computation.1 | async-start | bytes 6291456 | tf_op jit(solution)/shard_map/all_to_all | solution.py:68
  102.7 349.0 %reduce-scatter.6.cloned.1.call-start = ((), (), s32[]{:S(2)}) async-start(), calls=%async_computation.9 | async-start | bytes 5242880 | tf_op jit(solution)/shard_map/reduce_scatter | solution.py:55
  107.1 6.9 copy-start.44
  112.3 213.4 %collective-permute-start = (bf16[3,2048,384]{2,1,0:T(8,128)(2,1)}, bf16[3,2048,384]{2,1,0:T(8,128)(2,1)}, u32[]{:S(2)}, u32[]{:S(2)}) collective-permute-start(bf16[3,2048,384]{2,1,0:T(8,128)(2,1)} %pad_maximum_fusion), channel_id=1, source_target_pairs={{0,1},{1,0},{2,3},{3,2},{4,5},{5,4},{6,7},{7,6},{8,9},{9,8},{10,11... | collective-permute-start | bytes 14155784 | tf_op jit(solution)/shard_map/ppermute | solution.py:16
  348.0 5.7 copy-start.45
  348.0 5.7 copy-start.25
  357.1 74.0 %all-to-all-start.1 = ((bf16[32,24,2048]{2,1,0:T(8,128)(2,1)}), bf16[32,24,2048]{2,1,0:T(8,128)(2,1)}, u32[]{:S(2)}, u32[]{:S(2)}) async-start(bf16[32,24,2048]{2,1,0:T(8,128)(2,1)} %bitcast.132), calls=%async_computation.2 | async-start | bytes 6291456 | tf_op jit(solution)/shard_map/all_to_all | solution.py:72
  361.0 350.1 %all-gather.5.cloned.1.call-start = ((), (), s32[]{:S(2)}) async-start(), calls=%async_computation.10 | async-start | bytes 2621440 | tf_op jit(solution)/shard_map/all_gather | solution.py:64
  362.1 76.5 %copy-start.34 = (s32[1024]{0:T(1024)}, s32[1024]{0:T(1024)S(1)}, u32[]{:S(2)}) copy-start(s32[1024]{0:T(1024)S(1)} %pad_clamp_fusion) | copy-start | bytes 12292
  443.5 5.6 copy-start.8
  453.9 7.0 copy-start.42
  460.9 75.1 %copy-start.24 = (bf16[1,384,2048]{2,1,0:T(8,128)(2,1)S(1)}, bf16[1,384,2048]{2,1,0:T(8,128)(2,1)}, u32[]{:S(2)}) copy-start(bf16[1,384,2048]{2,1,0:T(8,128)(2,1)} %param.23) | copy-start | bytes 4718596
  460.9 75.1 %copy-start.48 = (f32[768,384]{1,0:T(8,128)S(1)}, f32[768,384]{1,0:T(8,128)}, u32[]{:S(2)}) copy-start(f32[768,384]{1,0:T(8,128)} %copy-done.47) | copy-start | bytes 3538948
  460.9 75.1 %copy-start.50 = (f32[768,384]{1,0:T(8,128)S(1)}, f32[768,384]{1,0:T(8,128)}, u32[]{:S(2)}) copy-start(f32[768,384]{1,0:T(8,128)} %get-tuple-element.45) | copy-start | bytes 3538948
  551.2 74.5 %copy-start.35 = (s32[1024]{0:T(1024)S(1)}, s32[1024]{0:T(1024)}, u32[]{:S(2)}) copy-start(s32[1024]{0:T(1024)} %copy-done.34) | copy-start | bytes 12292
  638.1 5.8 copy-start.38
  649.6 201.3 %all-gather.3.cloned.1.call-start = ((), (), s32[]{:S(2)}) async-start(), calls=%async_computation.8 | async-start | bytes 2621440 | tf_op jit(solution)/shard_map/all_gather | solution.py:64
  650.2 205.0 %reduce-scatter.8.cloned.1.call-start = ((), (), s32[]{:S(2)}) async-start(), calls=%async_computation.11 | async-start | bytes 4718592 | tf_op jit(solution)/shard_map/reduce_scatter | solution.py:190
  669.6 159.0 %collective-permute-start.1 = (bf16[3,2048,384]{2,1,0:T(8,128)(2,1)}, bf16[3,2048,384]{2,1,0:T(8,128)(2,1)}, u32[]{:S(2)}, u32[]{:S(2)}) collective-permute-start(bf16[3,2048,384]{2,1,0:T(8,128)(2,1)} %pad_maximum_fusion.1), channel_id=1, source_target_pairs={{0,1},{1,0},{2,3},{3,2},{4,5},{5,4},{6,7},{7,6},{8,9},{9,8},{10,11... | collective-permute-start | bytes 14155784 | tf_op jit(solution)/shard_map/ppermute | solution.py:16
  840.0 5.9 copy-start.10
  840.0 5.9 copy-start.11
  (37 other events, 111.3 us)
Sparse Core Ops, SparseCore 0:
  12.5 79.4 reduce-scatter.3
  118.0 142.1 reduce-scatter.5
  649.7 61.3 all-gather.4
  712.5 81.0 all-gather.2
  796.8 53.7 reduce-scatter.7
where the time goes:
time: 868 us; the launch traced here: 864 us
  waiting for transfers between devices  493 us (57%)
  blocking collectives  150 us (17%)
  matrix products  99 us (11%)
  local copies, waits for them, and re-layouts  54.7 us (6%)
  other arithmetic  38 us (4%)
  starting transfers between devices  14.6 us (2%)
  between operations  14.6 us (2%)
    ppermute x2, waiting for transfers between devices, swapped(): return lax.ppermute(block, axis, route)  310 us
    reduce_scatter x2, waiting for transfers between devices, tensor_rows(): lax.psum_scatter(jnp.dot(source, weights, preferred_element_type=jnp.floa...  76.7 us
    all_to_all x1, blocking collectives, dispatch_rows(): lax.all_to_all(payload, ('ctx', 'tp'), split_axis=0, concat_axis=0, tiled...  75.1 us
    all_to_all x1, blocking collectives, return_rows(): lax.all_to_all(payload, ('ctx', 'tp'), split_axis=0, concat_axis=0, tiled...  74.5 us
    all_to_all x1, waiting for transfers between devices, return_rows(): lax.all_to_all(payload, ('ctx', 'tp'), split_axis=0, concat_axis=0, tiled...  68.1 us
    all_gather x2, waiting for transfers between devices, group_rows(): return lax.all_gather(local_rows, 'tp', axis=0, tiled=True)  38.4 us
  transfers between devices with their start and end apart: 9, of which 5 were waited for; matrix products, arithmetic and copies ran while one was open for 15% of the time, Pallas kernels for 0%

commit v1 on v0

v1 whole, which is shorter than its diff:
```python
import jax
import jax.numpy as jnp
from jax import lax
from jax.sharding import PartitionSpec as P

EPSILON = 1e-06


def rms_inverse(hidden):
    return lax.rsqrt(jnp.mean(hidden * hidden, axis=-1, keepdims=True) + EPSILON)


def rms_grad(hidden, gain_vec, inv_rms, grad_out):
    normed = hidden * inv_rms
    grad_normed = grad_out * gain_vec
    return inv_rms * (grad_normed - normed * jnp.mean(grad_normed * normed, axis=-1, keepdims=True))


def expert_inner(slot_rows, gate_mat, up_mat):
    pre_gate = jnp.dot(slot_rows, gate_mat, preferred_element_type=jnp.float32)
    pre_up = jnp.dot(slot_rows, up_mat, preferred_element_type=jnp.float32)
    active = (jax.nn.silu(pre_gate) * pre_up).astype(jnp.bfloat16)
    return (pre_gate, pre_up, active)


def half_backward(slot_rows, slot_grads, pre_gate, pre_up, active, gate_mat, up_mat, down_mat):
    sigmoid_gate = jax.nn.sigmoid(pre_gate)
    silu_gate = pre_gate * sigmoid_gate
    grad_active = jnp.einsum("sd,fd->sf", slot_grads, down_mat, preferred_element_type=jnp.float32)
    grad_gate = (
        grad_active * pre_up * sigmoid_gate * (1.0 + pre_gate * (1.0 - sigmoid_gate))
    ).astype(jnp.bfloat16)
    grad_up = (grad_active * silu_gate).astype(jnp.bfloat16)
    input_part = jnp.einsum("sf,df->sd", grad_gate, gate_mat, preferred_element_type=jnp.float32)
    input_part = (
        input_part + jnp.einsum("sf,df->sd", grad_up, up_mat, preferred_element_type=jnp.float32)
    ).astype(jnp.bfloat16)
    gate_term = jnp.einsum("sd,sf->df", slot_rows, grad_gate, preferred_element_type=jnp.float32)
    up_term = jnp.einsum("sd,sf->df", slot_rows, grad_up, preferred_element_type=jnp.float32)
    down_term = jnp.einsum("sf,sd->fd", active, slot_grads, preferred_element_type=jnp.float32)
    return (input_part, gate_term, up_term, down_term)


def tensor_rows(local_sum):
    return lax.psum_scatter(
        local_sum.astype(jnp.bfloat16), "tp", scatter_dimension=0, tiled=True
    ).astype(jnp.float32)


def group_rows(local_rows):
    return lax.all_gather(local_rows, "tp", axis=0, tiled=True)


def exchange(blocks):
    return lax.all_to_all(blocks, "ctx", split_axis=0, concat_axis=0, tiled=True)


def local(
    attention,
    residual,
    w_out,
    w_qkv,
    norm_moe,
    norm_attn,
    expert_ids,
    expert_gates,
    w_gate,
    w_up,
    w_down,
    d_projected,
    d_stream,
):
    ctx_count = lax.axis_size("ctx")
    tensor_count = lax.axis_size("tp")
    group_tokens = attention.shape[0]
    local_tokens = group_tokens // tensor_count
    model_width = residual.shape[1]
    expert_count = ctx_count * tensor_count // 2
    top_count = expert_ids.shape[1]
    capacity = 2 * max(1, local_tokens * top_count * 3 // (4 * expert_count))
    group_cap = tensor_count * capacity
    slot_count = ctx_count * group_cap
    gate_mat = w_gate[0]
    up_mat = w_up[0]
    down_mat = w_down[0]

    routing = group_rows(
        jnp.concatenate([expert_ids.astype(jnp.float32), expert_gates], axis=1)
    )
    group_ids = routing[:, :top_count].astype(jnp.int32)
    group_gates = routing[:, top_count:]
    targets = (jnp.arange(ctx_count, dtype=jnp.int32) * tensor_count + lax.axis_index("tp")) // 2
    named = group_ids[:, None, :] == targets[None, :, None]
    member = jnp.any(named, axis=2)
    gate_of = jnp.sum(jnp.where(named, group_gates[:, None, :], 0.0), axis=2)
    token_range = jnp.arange(group_tokens, dtype=jnp.int32)
    earlier = (token_range[:, None] > token_range[None, :]).astype(jnp.bfloat16)
    position = jnp.dot(
        earlier, member.astype(jnp.bfloat16), preferred_element_type=jnp.float32
    ).astype(jnp.int32)
    slot_of = jnp.where(member, position, -1).T
    taken = slot_of[:, None, :] == jnp.arange(group_cap, dtype=jnp.int32)[None, :, None]
    select = taken.astype(jnp.bfloat16).reshape(slot_count, group_tokens)
    weighted = jnp.where(taken, gate_of.T[:, None, :], 0.0)
    slot_gate = jnp.sum(weighted, axis=2).reshape(slot_count, 1)
    weighted = weighted.astype(jnp.bfloat16).reshape(slot_count, group_tokens)

    def to_experts(rows):
        return exchange(rows.reshape(ctx_count, group_cap, model_width)).reshape(
            slot_count, model_width
        )

    grad_attn_in = tensor_rows(
        jnp.dot(d_projected, w_qkv, preferred_element_type=jnp.float32)
    )
    hidden = residual.astype(jnp.float32) + tensor_rows(
        jnp.dot(attention, w_out, preferred_element_type=jnp.float32)
    )
    inv_one = rms_inverse(hidden)
    moe_input = group_rows((hidden * inv_one * norm_moe).astype(jnp.bfloat16))
    arrived = to_experts(
        jnp.dot(select, moe_input, preferred_element_type=jnp.float32).astype(jnp.bfloat16)
    )
    pre_gate, pre_up, active = expert_inner(arrived, gate_mat, up_mat)
    half_out = jnp.dot(active, down_mat, preferred_element_type=jnp.float32).astype(jnp.bfloat16)
    returned = to_experts(half_out)
    moe_out = tensor_rows(
        jnp.einsum("st,sd->td", weighted, returned, preferred_element_type=jnp.float32)
    )
    stream_sum = hidden + moe_out
    stream = stream_sum.astype(jnp.bfloat16)
    inv_two = rms_inverse(stream_sum)
    grad_stream = d_stream.astype(jnp.float32) + rms_grad(
        stream_sum, norm_attn, inv_two, grad_attn_in
    )
    grad_rows = group_rows(grad_stream.astype(jnp.bfloat16))
    grad_slots = jnp.dot(select, grad_rows, preferred_element_type=jnp.float32) * slot_gate
    grad_arrived = to_experts(grad_slots.astype(jnp.bfloat16))
    attn_rows = group_rows((stream_sum * inv_two * norm_attn).astype(jnp.bfloat16))
    projected = jnp.einsum(
        "td,od->to", attn_rows, w_qkv, preferred_element_type=jnp.float32
    ).astype(jnp.bfloat16)
    input_part, gate_grad, up_grad, down_grad = half_backward(
        arrived, grad_arrived, pre_gate, pre_up, active, gate_mat, up_mat, down_mat
    )
    back_rows = to_experts(input_part)
    grad_moe_in = tensor_rows(
        jnp.einsum("st,sd->td", select, back_rows, preferred_element_type=jnp.float32)
    )
    grad_hidden = grad_stream + rms_grad(hidden, norm_moe, inv_one, grad_moe_in)
    grad_residual = grad_hidden.astype(jnp.bfloat16)
    grad_rows_all = group_rows(grad_residual)
    grad_attention = jnp.einsum(
        "td,kd->tk", grad_rows_all, w_out, preferred_element_type=jnp.float32
    ).astype(jnp.bfloat16)
    out_partial = jnp.einsum(
        "tk,td->kd", attention, grad_rows_all, preferred_element_type=jnp.float32
    )
    out_weight_grad = lax.psum_scatter(
        out_partial.astype(jnp.bfloat16), "ctx", scatter_dimension=1, tiled=True
    )
    return (
        projected,
        stream,
        grad_attention,
        grad_residual,
        out_weight_grad,
        gate_grad.astype(jnp.bfloat16)[None],
        up_grad.astype(jnp.bfloat16)[None],
        down_grad.astype(jnp.bfloat16)[None],
    )


def solution(mesh):
    in_specs = (
        P("ctx", "tp"),
        P(("ctx", "tp"), None),
        P("tp", None),
        P("tp", None),
        P(),
        P(),
        P(("ctx", "tp"), None),
        P(("ctx", "tp"), None),
        P(("ctx", "tp"), None, None),
        P(("ctx", "tp"), None, None),
        P(("ctx", "tp"), None, None),
        P("ctx", "tp"),
        P(("ctx", "tp"), None),
    )
    out_specs = (
        P("ctx", "tp"),
        P(("ctx", "tp"), None),
        P("ctx", "tp"),
        P(("ctx", "tp"), None),
        P("tp", "ctx"),
        P(("ctx", "tp"), None, None),
        P(("ctx", "tp"), None, None),
        P(("ctx", "tp"), None, None),
    )
    return jax.shard_map(local, mesh=mesh, in_specs=in_specs, out_specs=out_specs, check_vma=False)
```

time: 868 us -> 793 us (0.914)
  blocking collectives: 150 us -> 239 us
  waiting for transfers between devices: 493 us -> 419 us
  local copies, waits for them, and re-layouts: 54.7 us -> 2.08 us
  other arithmetic: 38 us -> 17.4 us
  matrix products: 99 us -> 89.1 us
  starting transfers between devices: 14.6 us -> 5.7 us
    ppermute x2 -> x0, waiting for transfers between devices: 310 us -> none  [swapped(): return lax.ppermute(block, axis, route)]
    reduce_scatter x3 -> x5, waiting for transfers between devices: 76.7 us -> 207 us  [the longest x4 168 us: tensor_rows(): lax.psum_scatter(local_sum.astype(jnp.bfloat16), 'tp', scatter_dimension=...]
    all_gather x2 -> x4, waiting for transfers between devices: 38.4 us -> 140 us  [group_rows(): return lax.all_gather(local_rows, 'tp', axis=0, tiled=True)]
    all_to_all x2 -> x3, blocking collectives: 150 us -> 226 us  [exchange(): lax.all_to_all(blocks, 'ctx', split_axis=0, concat_axis=0, tiled=True)]
    another operation x5 -> x0, local copies, waits for them, and re-layouts: 17.1 us -> none  [the longest x1 4.6 us: local(): down_grad = down_one + incoming[2].reshape(down_one.shape)]
    gather x2 -> x0, local copies, waits for them, and re-layouts: 15.1 us -> none  [the longest x1 7.55 us: local(): back_rows[slot_index].reshape(local_tokens, top_count, model_width)]
    all_gather x0 -> x1, blocking collectives: none -> 13.2 us  [group_rows(): return lax.all_gather(local_rows, 'tp', axis=0, tiled=True)]
    reduce_sum x4 -> x2, other arithmetic: 12.3 us -> 0.48 us  [the longest x1 0.4 us: local(): slot_gate = jnp.sum(weighted, axis=2).reshape(slot_count, 1)]
  transfers between devices with their start and end apart: 9 -> 10, of which waited for: 5 -> 10; matrix products, arithmetic and copies ran while one was open for 15% -> 5% of each run, Pallas kernels for 0% -> 0%
where the time goes in v1:
time: 793 us; the launch traced here: 787 us
  waiting for transfers between devices  419 us (53%)
  blocking collectives  239 us (30%)
  matrix products  89.1 us (11%)
  other arithmetic  17.4 us (2%)
  between operations  14.4 us (2%)
    all_to_all x3, blocking collectives, exchange(): lax.all_to_all(blocks, 'ctx', split_axis=0, concat_axis=0, tiled=True)  226 us
    reduce_scatter x4, waiting for transfers between devices, tensor_rows(): lax.psum_scatter(local_sum.astype(jnp.bfloat16), 'tp', scatter_dimension=...  168 us
    all_gather x4, waiting for transfers between devices, group_rows(): return lax.all_gather(local_rows, 'tp', axis=0, tiled=True)  140 us
    all_to_all x1, waiting for transfers between devices, exchange(): lax.all_to_all(blocks, 'ctx', split_axis=0, concat_axis=0, tiled=True)  71.5 us
    reduce_scatter x1, waiting for transfers between devices, local(): lax.psum_scatter(out_partial.astype(jnp.bfloat16), 'ctx', scatter_dimensi...  39 us
  transfers between devices with their start and end apart: 10, of which 10 were waited for; matrix products, arithmetic and copies ran while one was open for 5% of the time, Pallas kernels for 0%

profile of v1, /device:TPU:0, one launch (start us, length us, event | category | flops | bytes accessed | tf_op | source)
XLA Modules:
  0.0 787.1 jit_solution(12252560450946514049)
XLA Ops:
  11.8 46.7 %reduce-scatter.6.cloned.1.call-done = bf16[128,2048]{1,0:T(8,128)(2,1)} async-done(((bf16[512,2048]{1,0:T(8,128)(2,1)}), bf16[128,2048]{1,0:T(8,128)(2,1)}) %reduce-scatter.6.cloned.1.call-update) | async-done | bytes 524304 | tf_op jit(solution)/shard_map/reduce_scatter | solution.py:45
  62.3 13.2 %all_gather.15 = f32[512,8]{0,1:T(8,128)S(1)} all-gather(f32[128,8]{0,1:T(8,128)S(1)} %pad_maximum_fusion), channel_id=1, replica_groups=mesh['ctx'=8,'tp'=4] {'tp'}, dimensions={0}, use_global_device_ids=true | all-gather | bytes 20480 | tf_op jit(solution)/shard_map/all_gather | solution.py:51
  77.2 30.4 %all-gather.5.cloned.1.call-done = bf16[512,2048]{1,0:T(8,128)(2,1)} async-done(((bf16[128,2048]{1,0:T(8,128)(2,1)}), bf16[512,2048]{1,0:T(8,128)(2,1)}) %all-gather.5.cloned.1.call-update) | async-done | bytes 2097168 | tf_op jit(solution)/shard_map/all_gather | solution.py:51
  107.6 5.3 convolution_convert_fusion.1
  112.9 75.3 %all_to_all.20 = bf16[8,192,2048]{2,1,0:T(8,128)(2,1)S(1)} all-to-all(bf16[8,192,2048]{2,1,0:T(8,128)(2,1)S(1)} %bitcast.82), channel_id=1, replica_groups=mesh['ctx'=8,'tp'=4] {'ctx'}, dimensions={0} | all-to-all | bytes 12582912 | tf_op jit(solution)/shard_map/all_to_all | solution.py:55
  191.8 5.3 multiply_convert_fusion.3
  197.0 5.4 convolution_convert_fusion
  202.4 4.8 all-to-all-start.1
  207.3 71.5 %all-to-all-done.1 = bf16[8,192,2048]{2,1,0:T(8,128)(2,1)} async-done(((bf16[8,192,2048]{2,1,0:T(8,128)(2,1)}), bf16[8,192,2048]{2,1,0:T(8,128)(2,1)}, u32[]{:S(2)}, u32[]{:S(2)}) %all-to-all-start.1) | async-done | bytes 6291488 | tf_op jit(solution)/shard_map/all_to_all | solution.py:55
  278.7 7.4 bitcast_convert_fusion.1
  290.5 36.6 %reduce-scatter.8.cloned.1.call-done = bf16[128,2048]{1,0:T(8,128)(2,1)} async-done(((bf16[512,2048]{1,0:T(8,128)(2,1)}), bf16[128,2048]{1,0:T(8,128)(2,1)}) %reduce-scatter.8.cloned.1.call-update) | async-done | bytes 524304 | tf_op jit(solution)/shard_map/reduce_scatter | solution.py:45
  328.9 43.7 %reduce-scatter.10.cloned.1.call-done = bf16[128,2048]{1,0:T(8,128)(2,1)} async-done(((bf16[512,2048]{1,0:T(8,128)(2,1)}), bf16[128,2048]{1,0:T(8,128)(2,1)}) %reduce-scatter.10.cloned.1.call-update) | async-done | bytes 524304 | tf_op jit(solution)/shard_map/reduce_scatter | solution.py:45
  378.0 44.5 %all-gather.9.cloned.1.call-done = bf16[512,2048]{1,0:T(8,128)(2,1)} async-done(((bf16[128,2048]{1,0:T(8,128)(2,1)}), bf16[512,2048]{1,0:T(8,128)(2,1)}) %all-gather.9.cloned.1.call-update) | async-done | bytes 2097168 | tf_op jit(solution)/shard_map/all_gather | solution.py:51
  422.5 5.3 multiply_convert_fusion
  427.8 75.2 %all_to_all.21 = bf16[8,192,2048]{2,1,0:T(8,128)(2,1)S(1)} all-to-all(bf16[8,192,2048]{2,1,0:T(8,128)(2,1)S(1)} %bitcast.81), channel_id=1, replica_groups=mesh['ctx'=8,'tp'=4] {'ctx'}, dimensions={0} | all-to-all | bytes 12582912 | tf_op jit(solution)/shard_map/all_to_all | solution.py:55
  511.1 5.5 add_convert_fusion
  516.6 75.2 %all_to_all.22 = bf16[8,192,2048]{2,1,0:T(8,128)(2,1)S(1)} all-to-all(bf16[8,192,2048]{2,1,0:T(8,128)(2,1)} %bitcast.71), channel_id=1, replica_groups=mesh['ctx'=8,'tp'=4] {'ctx'}, dimensions={0} | all-to-all | bytes 12582912 | tf_op jit(solution)/shard_map/all_to_all | solution.py:55
  591.9 4.7 bitcast_convert_fusion
  596.6 40.9 %reduce-scatter.12.cloned.1.call-done = bf16[128,2048]{1,0:T(8,128)(2,1)} async-done(((bf16[512,2048]{1,0:T(8,128)(2,1)}), bf16[128,2048]{1,0:T(8,128)(2,1)}) %reduce-scatter.12.cloned.1.call-update) | async-done | bytes 524304 | tf_op jit(solution)/shard_map/reduce_scatter | solution.py:45
  644.1 44.4 %all-gather.11.cloned.1.call-done = bf16[512,2048]{1,0:T(8,128)(2,1)} async-done(((bf16[128,2048]{1,0:T(8,128)(2,1)}), bf16[512,2048]{1,0:T(8,128)(2,1)}) %all-gather.11.cloned.1.call-update) | async-done | bytes 2097168 | tf_op jit(solution)/shard_map/all_gather | solution.py:51
  692.9 7.2 fusion.3
  700.1 7.6 fusion.2
  714.3 21.0 %all-gather.7.cloned.1.call-done = bf16[512,2048]{1,0:T(8,128)(2,1)} async-done(((bf16[128,2048]{1,0:T(8,128)(2,1)}), bf16[512,2048]{1,0:T(8,128)(2,1)}) %all-gather.7.cloned.1.call-update) | async-done | bytes 2097168 | tf_op jit(solution)/shard_map/all_gather | solution.py:51
  739.6 39.0 %reduce-scatter.14.cloned.1.call-done = bf16[512,256]{0,1:T(8,128)(2,1)} async-done(((bf16[512,2048]{0,1:T(8,128)(2,1)}), bf16[512,256]{0,1:T(8,128)(2,1)}) %reduce-scatter.14.cloned.1.call-update) | async-done | bytes 262160 | tf_op jit(solution)/shard_map/reduce_scatter | solution.py:159
  (110 shorter events, 56.9 us)
Async XLA Ops:
  7.2 279.0 %copy-start = (bf16[768,2048]{1,0:T(8,128)(2,1)S(1)}, bf16[768,2048]{1,0:T(8,128)(2,1)}, u32[]{:S(2)}) copy-start(bf16[768,2048]{1,0:T(8,128)(2,1)} %param.16) | copy-start | bytes 9437188
  7.2 51.3 %reduce-scatter.6.cloned.1.call-start = ((), (), s32[]{:S(2)}) async-start(), calls=%async_computation.9 | async-start | bytes 2621440 | tf_op jit(solution)/shard_map/reduce_scatter | solution.py:45
  11.7 48.2 %copy-start.15 = (f32[2048]{0:T(1024)S(1)}, f32[2048]{0:T(1024)}, u32[]{:S(2)}) copy-start(f32[2048]{0:T(1024)} %param.17) | copy-start | bytes 24580
  11.7 50.5 %copy-start.17 = (s32[128,4]{0,1:T(4,128)S(1)}, s32[128,4]{0,1:T(4,128)}, u32[]{:S(2)}) copy-start(s32[128,4]{0,1:T(4,128)} %param.19) | copy-start | bytes 6148
  11.7 50.6 %copy-start.18 = (f32[128,4]{0,1:T(4,128)S(1)}, f32[128,4]{0,1:T(4,128)}, u32[]{:S(2)}) copy-start(f32[128,4]{0,1:T(4,128)} %param.20) | copy-start | bytes 6148
  11.8 95.8 %all-gather.5.cloned.1.call-start = ((), (), s32[]{:S(2)}) async-start(), calls=%async_computation.10 | async-start | bytes 2621440 | tf_op jit(solution)/shard_map/all_gather | solution.py:51
  112.9 75.3 %copy-start.7 = (bf16[1,2048,384]{2,1,0:T(8,128)(2,1)S(1)}, bf16[1,2048,384]{2,1,0:T(8,128)(2,1)}, u32[]{:S(2)}) copy-start(bf16[1,2048,384]{2,1,0:T(8,128)(2,1)} %param.21) | copy-start | bytes 4718596
  197.0 5.4 copy-start.23
  202.4 76.4 %all-to-all-start.1 = ((bf16[8,192,2048]{2,1,0:T(8,128)(2,1)}), bf16[8,192,2048]{2,1,0:T(8,128)(2,1)}, u32[]{:S(2)}, u32[]{:S(2)}) async-start(bf16[8,192,2048]{2,1,0:T(8,128)(2,1)} %bitcast.80), calls=%async_computation.2 | async-start | bytes 12582912 | tf_op jit(solution)/shard_map/all_to_all | solution.py:55
  207.1 120.0 %reduce-scatter.8.cloned.1.call-start = ((), (), s32[]{:S(2)}) async-start(), calls=%async_computation.11 | async-start | bytes 2621440 | tf_op jit(solution)/shard_map/reduce_scatter | solution.py:45
  286.2 86.4 %reduce-scatter.10.cloned.1.call-start = ((), (), s32[]{:S(2)}) async-start(), calls=%async_computation.13 | async-start | bytes 2621440 | tf_op jit(solution)/shard_map/reduce_scatter | solution.py:45
  290.5 82.1 %copy-start.16 = (f32[2048]{0:T(1024)S(1)}, f32[2048]{0:T(1024)}, u32[]{:S(2)}) copy-start(f32[2048]{0:T(1024)} %param.18) | copy-start | bytes 24580
  290.5 132.0 %all-gather.9.cloned.1.call-start = ((), (), s32[]{:S(2)}) async-start(), calls=%async_computation.14 | async-start | bytes 2621440 | tf_op jit(solution)/shard_map/all_gather | solution.py:51
  377.1 260.4 %reduce-scatter.12.cloned.1.call-start = ((), (), s32[]{:S(2)}) async-start(), calls=%async_computation.15 | async-start | bytes 2621440 | tf_op jit(solution)/shard_map/reduce_scatter | solution.py:45
  427.8 75.3 %copy-start.22 = (bf16[1,384,2048]{2,1,0:T(8,128)(2,1)S(1)}, bf16[1,384,2048]{2,1,0:T(8,128)(2,1)}, u32[]{:S(2)}) copy-start(bf16[1,384,2048]{2,1,0:T(8,128)(2,1)} %param.23) | copy-start | bytes 4718596
  427.8 75.3 %copy-start.25 = (f32[1536,384]{1,0:T(8,128)S(1)}, f32[1536,384]{1,0:T(8,128)}, u32[]{:S(2)}) copy-start(f32[1536,384]{1,0:T(8,128)} %copy-done.24) | copy-start | bytes 7077892
  427.8 75.3 %copy-start.26 = (f32[1536,384]{1,0:T(8,128)S(1)}, f32[1536,384]{1,0:T(8,128)}, u32[]{:S(2)}) copy-start(f32[1536,384]{1,0:T(8,128)} %get-tuple-element.32) | copy-start | bytes 7077892
  596.6 92.0 %all-gather.11.cloned.1.call-start = ((), (), s32[]{:S(2)}) async-start(), calls=%async_computation.16 | async-start | bytes 2621440 | tf_op jit(solution)/shard_map/all_gather | solution.py:51
  643.1 92.2 %all-gather.7.cloned.1.call-start = ((), (), s32[]{:S(2)}) async-start(), calls=%async_computation.12 | async-start | bytes 2621440 | tf_op jit(solution)/shard_map/all_gather | solution.py:51
  643.9 134.7 %reduce-scatter.14.cloned.1.call-start = ((), (), s32[]{:S(2)}) async-start(), calls=%async_computation.17 | async-start | bytes 2359296 | tf_op jit(solution)/shard_map/reduce_scatter | solution.py:159
  692.9 7.2 copy-start.14
  692.9 14.8 %slice-start = ((s8[6291456]{0:T(1024)(128)(4,1)}), s8[4194304]{0:T(1024)(128)(4,1)S(1)}, s32[]{:S(2)}) async-start(s8[6291456]{0:T(1024)(128)(4,1)} %bitcast.75), calls=%async_computation.18 | async-start | bytes 8388608
  700.0 7.6 slice-start.1
  700.0 7.6 copy-start.12
  (15 other events, 54.9 us)
Sparse Core Ops, SparseCore 0:
  11.9 46.5 reduce-scatter.5
  62.3 45.2 all-gather.4
  286.3 40.8 reduce-scatter.7
  329.3 43.1 reduce-scatter.9
  377.2 45.2 all-gather.8
  596.7 40.7 reduce-scatter.11
  643.2 45.2 all-gather.10
  690.7 44.5 all-gather.6
  738.6 39.9 reduce-scatter.13

commit v2 on v1

--- a/solution.py
+++ b/solution.py
@@ -1,7 +1,17 @@
+import functools
+
 import jax
 import jax.numpy as jnp
 from jax import lax
+from jax.experimental import pallas as pl
+from jax.experimental.pallas import tpu as pltpu
 from jax.sharding import PartitionSpec as P
+
+MESH = pl.DeviceIdType.MESH
+ROW_TILE = 16
+COLUMN_TILE = 512
+VMEM_BYTES = 40 * 1024 * 1024
+LINK_COST = 32
 
 EPSILON = 1e-06
 
@@ -51,8 +61,232 @@
     return lax.all_gather(local_rows, "tp", axis=0, tiled=True)
 
 
-def exchange(blocks):
-    return lax.all_to_all(blocks, "ctx", split_axis=0, concat_axis=0, tiled=True)
+def greet(ctx_count, tensor_count, me_ctx, me_tp):
+    barrier = pltpu.get_barrier_semaphore()
+    for k in range(1, tensor_count):
+        pl.semaphore_signal(
+            barrier, inc=1, device_id=(me_ctx, (me_tp + k) % tensor_count), device_id_type=MESH
+        )
+    for m in range(1, ctx_count):
+        pl.semaphore_signal(
+            barrier, inc=1, device_id=((me_ctx + m) % ctx_count, me_tp), device_id_type=MESH
+        )
+    pl.semaphore_wait(barrier, tensor_count + ctx_count - 2)
+
+
+def remote(src, dst, send_sem, recv_sem, device):
+    return pltpu.make_async_remote_copy(
+        src_ref=src,
+        dst_ref=dst,
+        send_sem=send_sem,
+        recv_sem=recv_sem,
+        device_id=device,
+        device_id_type=MESH,
+    )
+
+
+def dispatch_kernel(
+    ctx_count,
+    tensor_count,
+    cap,
+    rows_ref,
+    select_ref,
+    scale_ref,
+    out_ref,
+    gathered,
+    staged,
+    z_send,
+    z_recv,
+    p_send,
+    p_recv,
+    own_sem,
+):
+    me_ctx, me_tp = lax.axis_index("ctx"), lax.axis_index("tp")
+    width = rows_ref.shape[1]
+    tile = min(COLUMN_TILE, width)
+    greet(ctx_count, tensor_count, me_ctx, me_tp)
+    along = [
+        remote(
+            rows_ref,
+            gathered.at[k],
+            z_send.at[k],
+            z_recv.at[k],
+            (me_ctx, (me_tp + k) % tensor_count),
+        )
+        for k in range(1, tensor_count)
+    ]
+    for copy in along:
+        copy.start()
+    plane, own = [], []
+    for k in range(tensor_count):
+        if k > 0:
+            along[k - 1].wait_recv()
+        for start in range(0, width, tile):
+            columns = pl.ds(start, tile)
+            rows = rows_ref[:, columns] if k == 0 else gathered[k, :, columns]
+            picked = jnp.dot(select_ref[k], rows, preferred_element_type=jnp.float32)
+            staged[k, :, columns] = (picked * scale_ref[k]).astype(jnp.bfloat16)
+        for m in range(1, ctx_count):
+            span = pl.ds(m * cap, cap)
+            copy = remote(
+                staged.at[k, span],
+                out_ref.at[k, span],
+                p_send.at[k, m],
+                p_recv.at[k, m],
+                ((me_ctx + m) % ctx_count, me_tp),
+            )
+            copy.start()
+            plane.append(copy)
+        span = pl.ds(0, cap)
+        copy = pltpu.make_async_copy(staged.at[k, span], out_ref.at[k, span], own_sem.at[k])
+        copy.start()
+        own.append(copy)
+    for copy in along:
+        copy.wait_send()
+    for copy in plane + own:
+        copy.wait()
+
+
+def combine_kernel(
+    ctx_count,
+    tensor_count,
+    cap,
+    slots_ref,
+    weight_ref,
+    out_ref,
+    returned,
+    partial,
+    summed,
+    z_send,
+    z_recv,
+    p_send,
+    p_recv,
+    own_sem,
+):
+    me_ctx, me_tp = lax.axis_index("ctx"), lax.axis_index("tp")
+    width = out_ref.shape[1]
+    tile = min(COLUMN_TILE, width)
+    greet(ctx_count, tensor_count, me_ctx, me_tp)
+    order = list(range(tensor_count - 1, -1, -1))
+    plane, own = {}, {}
+    for k in order:
+        plane[k] = []
+        for m in range(1, ctx_count):
+            span = pl.ds(m * cap, cap)
+            copy = remote(
+                slots_ref.at[k, span],
+                returned.at[k, span],
+                p_send.at[k, m],
+                p_recv.at[k, m],
+                ((me_ctx + ctx_count - m) % ctx_count, me_tp),
+            )
+            copy.start()
+            plane[k].append(copy)
+        span = pl.ds(0, cap)
+        own[k] = pltpu.make_async_copy(
+            slots_ref.at[k, span], returned.at[k, span], own_sem.at[k]
+        )
+        own[k].start()
+    along = []
+    for k in order:
+        for copy in plane[k]:
+            copy.wait_recv()
+        own[k].wait()
+        for start in range(0, width, tile):
+            columns = pl.ds(start, tile)
+            total = jnp.dot(
+                weight_ref[k], returned[k, :, columns], preferred_element_type=jnp.float32
+            )
+            if k == 0:
+                out_ref[:, columns] = total
+            else:
+                partial[k, :, columns] = total.astype(jnp.bfloat16)
+        if k > 0:
+            copy = remote(
+                partial.at[k],
+                summed.at[k],
+                z_send.at[k],
+                z_recv.at[k],
+                (me_ctx, (me_tp + tensor_count - k) % tensor_count),
+            )
+            copy.start()
+            along.append(copy)
+    for copy in along:
+        copy.wait_recv()
+    for start in range(0, width, tile):
+        columns = pl.ds(start, tile)
+        total = out_ref[:, columns]
+        for k in range(1, tensor_count):
+            total = total + summed[k, :, columns].astype(jnp.float32)
+        out_ref[:, columns] = total
+    for copy in along:
+        copy.wait_send()
+    for k in order:
+        for copy in plane[k]:
+            copy.wait_send()
+
+
+def semaphores(ctx_count, tensor_count):
+    return [
+        pltpu.SemaphoreType.DMA((tensor_count,)),
+        pltpu.SemaphoreType.DMA((tensor_count,)),
+        pltpu.SemaphoreType.DMA((tensor_count, ctx_count)),
+        pltpu.SemaphoreType.DMA((tensor_count, ctx_count)),
+        pltpu.SemaphoreType.DMA((tensor_count,)),
+    ]
+
+
+def estimate(slots, tokens, width):
+    return pl.CostEstimate(
+        flops=2 * slots * tokens * width,
+        bytes_accessed=2 * slots * width * LINK_COST,
+        transcendentals=0,
+    )
+
+
+def dispatch(rows, select, scale, cap):
+    ctx_count, tensor_count = lax.axis_size("ctx"), lax.axis_size("tp")
+    tokens, width = rows.shape
+    slots = select.shape[1]
+    vmem = pl.BlockSpec(memory_space=pltpu.VMEM)
+    return pl.pallas_call(
+        functools.partial(dispatch_kernel, ctx_count, tensor_count, cap),
+        out_shape=jax.ShapeDtypeStruct((tensor_count, slots, width), jnp.bfloat16),
+        in_specs=[vmem] * 3,
+        out_specs=pl.BlockSpec(memory_space=pl.ANY),
+        scratch_shapes=[
+            pltpu.VMEM((tensor_count, tokens, width), jnp.bfloat16),
+            pltpu.VMEM((tensor_count, slots, width), jnp.bfloat16),
+        ]
+        + semaphores(ctx_count, tensor_count),
+        compiler_params=pltpu.CompilerParams(
+            collective_id=0, has_side_effects=True, vmem_limit_bytes=VMEM_BYTES
+        ),
+        cost_estimate=estimate(tensor_count * slots, tokens, width),
+    )(rows, select, scale)
+
+
+def combine(slot_rows, weights, cap):
+    ctx_count, tensor_count = lax.axis_size("ctx"), lax.axis_size("tp")
+    tokens, slots = weights.shape[1:]
+    width = slot_rows.shape[2]
+    vmem = pl.BlockSpec(memory_space=pltpu.VMEM)
+    return pl.pallas_call(
+        functools.partial(combine_kernel, ctx_count, tensor_count, cap),
+        out_shape=jax.ShapeDtypeStruct((tokens, width), jnp.float32),
+        in_specs=[pl.BlockSpec(memory_space=pl.ANY), vmem],
+        out_specs=vmem,
+        scratch_shapes=[
+            pltpu.VMEM((tensor_count, slots, width), jnp.bfloat16),
+            pltpu.VMEM((tensor_count, tokens, width), jnp.bfloat16),
+            pltpu.VMEM((tensor_count, tokens, width), jnp.bfloat16),
+        ]
+        + semaphores(ctx_count, tensor_count),
+        compiler_params=pltpu.CompilerParams(
+            collective_id=1, has_side_effects=True, vmem_limit_bytes=VMEM_BYTES
+        ),
+        cost_estimate=estimate(tensor_count * slots, tokens, width),
+    )(slot_rows, weights)
 
 
 def local(
@@ -72,81 +306,83 @@
 ):
     ctx_count = lax.axis_size("ctx")
     tensor_count = lax.axis_size("tp")
-    group_tokens = attention.shape[0]
-    local_tokens = group_tokens // tensor_count
+    local_tokens = residual.shape[0]
     model_width = residual.shape[1]
     expert_count = ctx_count * tensor_count // 2
     top_count = expert_ids.shape[1]
     capacity = 2 * max(1, local_tokens * top_count * 3 // (4 * expert_count))
-    group_cap = tensor_count * capacity
-    slot_count = ctx_count * group_cap
+    cap = -(-capacity // ROW_TILE) * ROW_TILE
+    slots = ctx_count * cap
+    me_ctx, me_tp = lax.axis_index("ctx"), lax.axis_index("tp")
     gate_mat = w_gate[0]
     up_mat = w_up[0]
     down_mat = w_down[0]
 
-    routing = group_rows(
-        jnp.concatenate([expert_ids.astype(jnp.float32), expert_gates], axis=1)
-    )
-    group_ids = routing[:, :top_count].astype(jnp.int32)
-    group_gates = routing[:, top_count:]
-    targets = (jnp.arange(ctx_count, dtype=jnp.int32) * tensor_count + lax.axis_index("tp")) // 2
-    named = group_ids[:, None, :] == targets[None, :, None]
-    member = jnp.any(named, axis=2)
-    gate_of = jnp.sum(jnp.where(named, group_gates[:, None, :], 0.0), axis=2)
-    token_range = jnp.arange(group_tokens, dtype=jnp.int32)
-    earlier = (token_range[:, None] > token_range[None, :]).astype(jnp.bfloat16)
+    routing = jnp.concatenate([expert_ids.astype(jnp.float32), expert_gates], axis=1)
+    blocks = jnp.stack(
+        [routing]
+        + [
+            lax.ppermute(
+                routing, "tp", [(i, (i + k) % tensor_count) for i in range(tensor_count)]
+            )
+            for k in range(1, tensor_count)
+        ]
+    )
+    ids = blocks[:, :, :top_count].astype(jnp.int32)
+    gates = blocks[:, :, top_count:]
+    peers = (me_ctx + jnp.arange(ctx_count, dtype=jnp.int32)) % ctx_count
+    targets = (peers * tensor_count + me_tp) // 2
+    named = ids[:, None, :, :] == targets[None, :, None, None]
+    member = jnp.any(named, axis=3)
+    gate_of = jnp.sum(jnp.where(named, gates[:, None, :, :], 0.0), axis=3)
+    token_range = jnp.arange(local_tokens, dtype=jnp.int32)
+    earlier = (token_range[:, None] < token_range[None, :]).astype(jnp.bfloat16)
     position = jnp.dot(
-        earlier, member.astype(jnp.bfloat16), preferred_element_type=jnp.float32
+        member.astype(jnp.bfloat16), earlier, preferred_element_type=jnp.float32
     ).astype(jnp.int32)
-    slot_of = jnp.where(member, position, -1).T
-    taken = slot_of[:, None, :] == jnp.arange(group_cap, dtype=jnp.int32)[None, :, None]
-    select = taken.astype(jnp.bfloat16).reshape(slot_count, group_tokens)
-    weighted = jnp.where(taken, gate_of.T[:, None, :], 0.0)
-    slot_gate = jnp.sum(weighted, axis=2).reshape(slot_count, 1)
-    weighted = weighted.astype(jnp.bfloat16).reshape(slot_count, group_tokens)
-
-    def to_experts(rows):
-        return exchange(rows.reshape(ctx_count, group_cap, model_width)).reshape(
-            slot_count, model_width
-        )
-
+    slot_of = jnp.where(member, position, -1)
+    taken = slot_of[:, :, None, :] == jnp.arange(cap, dtype=jnp.int32)[None, None, :, None]
+    select = taken.astype(jnp.bfloat16).reshape(tensor_count, slots, local_tokens)
+    slot_gate = jnp.sum(jnp.where(taken, gate_of[:, :, None, :], 0.0), axis=3)
+    slot_gate = slot_gate.reshape(tensor_count, slots, 1)
+    select_back = jnp.swapaxes(select, 1, 2)
+    gated_back = select_back * jnp.swapaxes(slot_gate, 1, 2).astype(jnp.bfloat16)
+
+    def flat(rows):
+        return rows.reshape(tensor_count * slots, model_width)
+
+    def blocked(rows):
+        return rows.reshape(tensor_count, slots, model_width)
+
+    hidden = residual.astype(jnp.float32) + tensor_rows(
+        jnp.dot(attention, w_out, preferred_element_type=jnp.float32)
+    )
+    inv_one = rms_inverse(hidden)
+    moe_input = (hidden * inv_one * norm_moe).astype(jnp.bfloat16)
+    moe_input, d_projected = lax.optimization_barrier((moe_input, d_projected))
     grad_attn_in = tensor_rows(
         jnp.dot(d_projected, w_qkv, preferred_element_type=jnp.float32)
     )
-    hidden = residual.astype(jnp.float32) + tensor_rows(
-        jnp.dot(attention, w_out, preferred_element_type=jnp.float32)
-    )
-    inv_one = rms_inverse(hidden)
-    moe_input = group_rows((hidden * inv_one * norm_moe).astype(jnp.bfloat16))
-    arrived = to_experts(
-        jnp.dot(select, moe_input, preferred_element_type=jnp.float32).astype(jnp.bfloat16)
-    )
+    arrived = flat(dispatch(moe_input, select, jnp.ones_like(slot_gate), cap))
     pre_gate, pre_up, active = expert_inner(arrived, gate_mat, up_mat)
     half_out = jnp.dot(active, down_mat, preferred_element_type=jnp.float32).astype(jnp.bfloat16)
-    returned = to_experts(half_out)
-    moe_out = tensor_rows(
-        jnp.einsum("st,sd->td", weighted, returned, preferred_element_type=jnp.float32)
-    )
-    stream_sum = hidden + moe_out
+    half_out, grad_attn_in = lax.optimization_barrier((half_out, grad_attn_in))
+    stream_sum = hidden + combine(blocked(half_out), gated_back, cap)
     stream = stream_sum.astype(jnp.bfloat16)
     inv_two = rms_inverse(stream_sum)
     grad_stream = d_stream.astype(jnp.float32) + rms_grad(
         stream_sum, norm_attn, inv_two, grad_attn_in
     )
-    grad_rows = group_rows(grad_stream.astype(jnp.bfloat16))
-    grad_slots = jnp.dot(select, grad_rows, preferred_element_type=jnp.float32) * slot_gate
-    grad_arrived = to_experts(grad_slots.astype(jnp.bfloat16))
     attn_rows = group_rows((stream_sum * inv_two * norm_attn).astype(jnp.bfloat16))
+    grad_arrived = flat(dispatch(grad_stream.astype(jnp.bfloat16), select, slot_gate, cap))
+    input_part, gate_grad, up_grad, down_grad = half_backward(
+        arrived, grad_arrived, pre_gate, pre_up, active, gate_mat, up_mat, down_mat
+    )
+    input_part, attn_rows = lax.optimization_barrier((input_part, attn_rows))
     projected = jnp.einsum(
         "td,od->to", attn_rows, w_qkv, preferred_element_type=jnp.float32
     ).astype(jnp.bfloat16)
-    input_part, gate_grad, up_grad, down_grad = half_backward(
-        arrived, grad_arrived, pre_gate, pre_up, active, gate_mat, up_mat, down_mat
-    )
-    back_rows = to_experts(input_part)
-    grad_moe_in = tensor_rows(
-        jnp.einsum("st,sd->td", select, back_rows, preferred_element_type=jnp.float32)
-    )
+    grad_moe_in = combine(blocked(input_part), select_back, cap)
     grad_hidden = grad_stream + rms_grad(hidden, norm_moe, inv_one, grad_moe_in)
     grad_residual = grad_hidden.astype(jnp.bfloat16)
     grad_rows_all = group_rows(grad_residual)
@@ -157,8 +393,8 @@
         "tk,td->kd", attention, grad_rows_all, preferred_element_type=jnp.float32
     )
     out_weight_grad = lax.psum_scatter(
-        out_partial.astype(jnp.bfloat16), "ctx", scatter_dimension=1, tiled=True
-    )
+        out_partial, "ctx", scatter_dimension=1, tiled=True
+    ).astype(jnp.bfloat16)
     return (
         projected,
         stream,

time: 793 us -> 612 us (0.77)
  Pallas kernels: 0 us -> 371 us
  waiting for transfers between devices: 419 us -> 117 us
  blocking collectives: 239 us -> 0 us
  matrix products: 89.1 us -> 64.5 us
  local copies, waits for them, and re-layouts: 2.08 us -> 21.5 us
    pallas_call x0 -> x4, Pallas kernels: none -> 371 us  [the longest x2 186 us: dispatch(): pl.pallas_call(functools.partial(dispatch_kernel, ctx_count, tensor_count...]
    all_to_all x3 -> x0, blocking collectives: 226 us -> none  [exchange(): lax.all_to_all(blocks, 'ctx', split_axis=0, concat_axis=0, tiled=True)]
    reduce_scatter x4 -> x2, waiting for transfers between devices: 168 us -> 46.7 us  [tensor_rows(): lax.psum_scatter(local_sum.astype(jnp.bfloat16), 'tp', scatter_dimension=...]
    all_gather x4 -> x2, waiting for transfers between devices: 140 us -> 44.2 us  [group_rows(): return lax.all_gather(local_rows, 'tp', axis=0, tiled=True)]
    all_to_all x1 -> x0, waiting for transfers between devices: 71.5 us -> none  [exchange(): lax.all_to_all(blocks, 'ctx', split_axis=0, concat_axis=0, tiled=True)]
    dot_general x5 -> x1, matrix products: 22.8 us -> 0.14 us  [local(): jnp.dot(member.astype(jnp.bfloat16), earlier, preferred_element_type=jnp....]
    reduce_scatter x1, waiting for transfers between devices: 39 us -> 25.1 us  [local(): lax.psum_scatter(out_partial, 'ctx', scatter_dimension=1, tiled=True)]
    unnamed x59 -> x105, local copies, waits for them, and re-layouts: 1.93 us -> 15.6 us
  transfers between devices with their start and end apart: 10 -> 8, of which waited for: 10 -> 4; matrix products, arithmetic and copies ran while one was open for 5% -> 10% of each run, Pallas kernels for 0% -> 31%
where the time goes in v2:
time: 612 us; the launch traced here: 608 us
  Pallas kernels  371 us (61%)
  waiting for transfers between devices  117 us (19%)
  matrix products  64.5 us (11%)
  local copies, waits for them, and re-layouts  21.5 us (4%)
  between operations  14.5 us (2%)
  other arithmetic  13.3 us (2%)
    pallas_call x2, Pallas kernels, dispatch(): pl.pallas_call(functools.partial(dispatch_kernel, ctx_count, tensor_count...  186 us
    pallas_call x2, Pallas kernels, combine(): pl.pallas_call(functools.partial(combine_kernel, ctx_count, tensor_count,...  185 us
    reduce_scatter x2, waiting for transfers between devices, tensor_rows(): lax.psum_scatter(local_sum.astype(jnp.bfloat16), 'tp', scatter_dimension=...  46.7 us
    all_gather x2, waiting for transfers between devices, group_rows(): return lax.all_gather(local_rows, 'tp', axis=0, tiled=True)  44.2 us
    reduce_scatter x1, waiting for transfers between devices, local(): lax.psum_scatter(out_partial, 'ctx', scatter_dimension=1, tiled=True)  25.1 us
    unnamed x105, local copies, waits for them, and re-layouts  15.6 us
  transfers between devices with their start and end apart: 8, of which 4 were waited for; matrix products, arithmetic and copies ran while one was open for 10% of the time, Pallas kernels for 31%

profile of v2, /device:TPU:0, one launch (start us, length us, event | category | flops | bytes accessed | tf_op | source)
XLA Modules:
  0.0 608.1 jit_solution(5698707278460551815)
XLA Ops:
  7.2 4.5 convolution_convert_fusion.2
  11.8 46.7 %reduce-scatter.4.cloned.1.call-done = bf16[128,2048]{1,0:T(8,128)(2,1)} async-done(((bf16[512,2048]{1,0:T(8,128)(2,1)}), bf16[128,2048]{1,0:T(8,128)(2,1)}) %reduce-scatter.4.cloned.1.call-update) | async-done | bytes 524304 | tf_op jit(solution)/shard_map/reduce_scatter | solution.py:55
  62.7 3.1 convolution_convert_fusion.1
  68.7 3.7 collective-permute-start.2
  75.6 2.3 copy.34
  82.4 94.6 %shard_map.188 = bf16[4,384,2048]{2,1,0:T(8,128)(2,1)S(1)} custom-call(bf16[128,2048]{1,0:T(8,128)(2,1)S(1)} %copy-done.7, bf16[4,384,128]{2,1,0:T(8,128)(2,1)S(1)} %copy.35.select_ref, f32[4,384,1]{2,1,0:T(8,128)S(1)} %broadcast_in_dim.37.scale_ref), custom_call_target="tpu_custom_call" | custom-call | flops 805306368 | bytes 201326592 | tf_op jit(solution)/shard_map/pallas_call | solution.py:252
  177.0 3.4 fusion.12
  180.5 5.0 multiply_convert_fusion.2
  186.6 5.3 convolution_convert_fusion
  193.1 3.2 copy-done.4
  197.2 85.2 %shard_map.189 = f32[128,2048]{1,0:T(8,128)S(1)} custom-call(bf16[4,384,2048]{2,1,0:T(8,128)(2,1)S(1)} %bitcast.74, bf16[4,128,384]{2,1,0:T(8,128)(2,1)S(1)} %copy-done.9), custom_call_target="tpu_custom_call" | custom-call | flops 805306368 | bytes 201326592 | tf_op jit(solution)/shard_map/pallas_call | solution.py:274
  289.7 91.8 %shard_map.190 = bf16[4,384,2048]{2,1,0:T(8,128)(2,1)S(1)} custom-call(bf16[128,2048]{1,0:T(8,128)(2,1)S(1)} %copy-done.8, bf16[4,384,128]{2,1,0:T(8,128)(2,1)S(1)} %copy.35.select_ref, f32[4,384,1]{2,1,0:T(8,128)S(1)} %copy-done.6), custom_call_target="tpu_custom_call" | custom-call | flops 805306368 | bytes 201326592 | tf_op jit(solution)/shard_map/pallas_call | solution.py:252
  381.6 4.2 multiply_convert_fusion
  385.8 3.5 fusion.10
  389.4 5.5 add_convert_fusion
  394.9 2.8 copy-done.1
  397.7 99.4 %shard_map.191 = f32[128,2048]{1,0:T(8,128)S(1)} custom-call(bf16[4,384,2048]{2,1,0:T(8,128)(2,1)S(1)} %bitcast.65, bf16[4,128,384]{2,1,0:T(8,128)(2,1)S(1)} %bitcast.75), custom_call_target="tpu_custom_call" | custom-call | flops 805306368 | bytes 201326592 | tf_op jit(solution)/shard_map/pallas_call | solution.py:274
  500.2 44.2 %all-gather.5.cloned.1.call-done = bf16[512,2048]{1,0:T(8,128)(2,1)} async-done(((bf16[128,2048]{1,0:T(8,128)(2,1)}), bf16[512,2048]{1,0:T(8,128)(2,1)}) %all-gather.5.cloned.1.call-update) | async-done | bytes 2097168 | tf_op jit(solution)/shard_map/all_gather | solution.py:61
  544.4 4.9 convolution_bitcast_fusion
  549.3 7.1 %fusion.2 = bf16[1,384,2048]{2,1,0:T(8,128)(2,1)} fusion(bf16[1536,384]{1,0:T(8,128)(2,1)} %copy-done.46, bf16[1536,2048]{1,0:T(8,128)(2,1)} %bitcast.73), kind=kOutput, calls=%fused_computation.10 | convolution fusion | flops 2416705536 | bytes 9043968 | tf_op jit(solution)/shard_map/sf,sd->fd/dot_general | solution.py:50
  556.4 8.2 %fusion.1 = bf16[1,2048,384]{2,1,0:T(8,128)(2,1)} fusion(bf16[1536,2048]{1,0:T(8,128)(2,1)} %bitcast.68, bf16[1536,384]{1,0:T(8,128)(2,1)S(1)} %copy-done.28), kind=kOutput, calls=%fused_computation.9 | convolution fusion | flops 2416705536 | bytes 9043968 | tf_op jit(solution)/shard_map/sd,sf->df/dot_general | solution.py:49
  564.6 4.7 fusion
  569.4 2.8 convolution_convert_fusion.6
  574.4 25.1 %reduce-scatter.8.cloned.1.call-done = f32[512,256]{0,1:T(8,128)} async-done(((f32[512,2048]{0,1:T(8,128)}), f32[512,256]{0,1:T(8,128)}) %reduce-scatter.8.cloned.1.call-update) | async-done | bytes 524304 | tf_op jit(solution)/shard_map/reduce_scatter | solution.py:395
  (154 shorter events, 32.6 us)
Async XLA Ops:
  7.2 55.6 %copy-start = (bf16[768,2048]{1,0:T(8,128)(2,1)S(1)}, bf16[768,2048]{1,0:T(8,128)(2,1)}, u32[]{:S(2)}) copy-start(bf16[768,2048]{1,0:T(8,128)(2,1)} %param.16) | copy-start | bytes 9437188
  7.2 51.3 %reduce-scatter.4.cloned.1.call-start = ((), (), s32[]{:S(2)}) async-start(), calls=%async_computation.3 | async-start | bytes 2621440 | tf_op jit(solution)/shard_map/reduce_scatter | solution.py:55
  11.7 48.8 %copy-start.29 = (f32[2048]{0:T(1024)S(1)}, f32[2048]{0:T(1024)}, u32[]{:S(2)}) copy-start(f32[2048]{0:T(1024)} %param.17) | copy-start | bytes 24580
  11.7 180.1 %reduce-scatter.6.cloned.1.call-start = ((), (), s32[]{:S(2)}) async-start(), calls=%async_computation.4 | async-start | bytes 2621440 | tf_op jit(solution)/shard_map/reduce_scatter | solution.py:55
  65.9 329.0 %all-gather.3.cloned.1.call-start = ((), (), s32[]{:S(2)}) async-start(), calls=%async_computation.5 | async-start | bytes 2621440 | tf_op jit(solution)/shard_map/all_gather | solution.py:61
  66.6 5.9 collective-permute-start.1
  68.4 5.5 collective-permute-start
  68.7 5.2 collective-permute-start.2
  82.4 94.6 %copy-start.21 = (bf16[1,2048,384]{2,1,0:T(8,128)(2,1)S(1)}, bf16[1,2048,384]{2,1,0:T(8,128)(2,1)}, u32[]{:S(2)}) copy-start(bf16[1,2048,384]{2,1,0:T(8,128)(2,1)} %param.21) | copy-start | bytes 4718596
  193.0 90.9 %copy-start.12 = (f32[128,2048]{1,0:T(8,128)}, f32[128,2048]{1,0:T(8,128)S(1)}, u32[]{:S(2)}) copy-start(f32[128,2048]{1,0:T(8,128)S(1)} %convert_element_type.104) | copy-start | bytes 3145732
  197.2 85.2 %copy-start.14 = (bf16[128,2048]{1,0:T(8,128)(2,1)S(1)}, bf16[128,2048]{1,0:T(8,128)(2,1)}, u32[]{:S(2)}) copy-start(bf16[128,2048]{1,0:T(8,128)(2,1)} %param.14) | copy-start | bytes 1572868
  197.2 85.2 %copy-start.16 = (bf16[128,2048]{1,0:T(8,128)(2,1)S(1)}, bf16[128,2048]{1,0:T(8,128)(2,1)}, u32[]{:S(2)}) copy-start(bf16[128,2048]{1,0:T(8,128)(2,1)} %reduce-scatter.4.cloned.1.call-done) | copy-start | bytes 1572868
  286.2 258.1 %all-gather.5.cloned.1.call-start = ((), (), s32[]{:S(2)}) async-start(), calls=%async_computation.6 | async-start | bytes 2621440 | tf_op jit(solution)/shard_map/all_gather | solution.py:61
  289.7 91.8 %copy-start.44 = (bf16[1,384,2048]{2,1,0:T(8,128)(2,1)S(1)}, bf16[1,384,2048]{2,1,0:T(8,128)(2,1)}, u32[]{:S(2)}) copy-start(bf16[1,384,2048]{2,1,0:T(8,128)(2,1)} %param.23) | copy-start | bytes 4718596
  289.7 91.8 %copy-start.48 = (f32[1536,384]{1,0:T(8,128)S(1)}, f32[1536,384]{1,0:T(8,128)}, u32[]{:S(2)}) copy-start(f32[1536,384]{1,0:T(8,128)} %copy-done.47) | copy-start | bytes 7077892
  289.7 91.8 %copy-start.49 = (f32[1536,384]{1,0:T(8,128)S(1)}, f32[1536,384]{1,0:T(8,128)}, u32[]{:S(2)}) copy-start(f32[1536,384]{1,0:T(8,128)} %get-tuple-element.57) | copy-start | bytes 7077892
  397.7 99.4 %copy-start.15 = (bf16[128,2048]{1,0:T(8,128)(2,1)S(1)}, bf16[128,2048]{1,0:T(8,128)(2,1)}, u32[]{:S(2)}) copy-start(bf16[128,2048]{1,0:T(8,128)(2,1)} %param.14) | copy-start | bytes 1572868
  397.7 99.4 %copy-start.17 = (bf16[128,2048]{1,0:T(8,128)(2,1)S(1)}, bf16[128,2048]{1,0:T(8,128)(2,1)}, u32[]{:S(2)}) copy-start(bf16[128,2048]{1,0:T(8,128)(2,1)} %reduce-scatter.4.cloned.1.call-done) | copy-start | bytes 1572868
  397.7 99.4 %copy-start.30 = (f32[2048]{0:T(1024)S(1)}, f32[2048]{0:T(1024)}, u32[]{:S(2)}) copy-start(f32[2048]{0:T(1024)} %param.17) | copy-start | bytes 24580
  397.7 99.4 %copy-start.34 = (f32[128]{0:T(128)S(1)}, f32[128]{0:T(128)}, u32[]{:S(2)}) copy-start(f32[128]{0:T(128)} %copy-done.33) | copy-start | bytes 1540
  397.7 99.8 %copy-start.20 = (bf16[128,2048]{1,0:T(8,128)(2,1)S(1)}, bf16[128,2048]{1,0:T(8,128)(2,1)}, u32[]{:S(2)}) copy-start(bf16[128,2048]{1,0:T(8,128)(2,1)} %param.25) | copy-start | bytes 1572868
  500.1 99.3 %reduce-scatter.8.cloned.1.call-start = ((), (), s32[]{:S(2)}) async-start(), calls=%async_computation.7 | async-start | bytes 4718592 | tf_op jit(solution)/shard_map/reduce_scatter | solution.py:395
  549.3 15.3 %slice-start = ((s8[6291456]{0:T(1024)(128)(4,1)}), s8[4194304]{0:T(1024)(128)(4,1)S(1)}, s32[]{:S(2)}) async-start(s8[6291456]{0:T(1024)(128)(4,1)} %bitcast.69), calls=%async_computation.8 | async-start | bytes 8388608
  556.4 8.2 %copy-start.26 = (bf16[1536,384]{1,0:T(8,128)(2,1)S(1)}, bf16[1536,384]{1,0:T(8,128)(2,1)}, u32[]{:S(2)}) copy-start(bf16[1536,384]{1,0:T(8,128)(2,1)} %copy-done.25) | copy-start | bytes 3538948
  (36 other events, 102.5 us)
Sparse Core Ops, SparseCore 0:
  11.9 46.5 reduce-scatter.3
  66.0 70.8 reduce-scatter.5
  286.3 80.9 all-gather.2
  500.3 44.0 all-gather.4
  549.4 50.0 reduce-scatter.7

commit v3 on v2

--- a/solution.py
+++ b/solution.py
@@ -72,6 +72,10 @@
             barrier, inc=1, device_id=((me_ctx + m) % ctx_count, me_tp), device_id_type=MESH
         )
     pl.semaphore_wait(barrier, tensor_count + ctx_count - 2)
+
+
+def near_first(tensor_count):
+    return sorted(range(1, tensor_count), key=lambda k: (min(k, tensor_count - k), k))
 
 
 def remote(src, dst, send_sem, recv_sem, device):
@@ -105,8 +109,8 @@
     width = rows_ref.shape[1]
     tile = min(COLUMN_TILE, width)
     greet(ctx_count, tensor_count, me_ctx, me_tp)
-    along = [
-        remote(
+    along = {
+        k: remote(
             rows_ref,
             gathered.at[k],
             z_send.at[k],
@@ -114,13 +118,14 @@
             (me_ctx, (me_tp + k) % tensor_count),
         )
         for k in range(1, tensor_count)
-    ]
-    for copy in along:
-        copy.start()
+    }
+    order = [0] + near_first(tensor_count)
     plane, own = [], []
-    for k in range(tensor_count):
+    for turn, k in enumerate(order):
         if k > 0:
-            along[k - 1].wait_recv()
+            along[k].wait()
+        if turn + 1 < tensor_count:
+            along[order[turn + 1]].start()
         for start in range(0, width, tile):
             columns = pl.ds(start, tile)
             rows = rows_ref[:, columns] if k == 0 else gathered[k, :, columns]
@@ -141,8 +146,6 @@
         copy = pltpu.make_async_copy(staged.at[k, span], out_ref.at[k, span], own_sem.at[k])
         copy.start()
         own.append(copy)
-    for copy in along:
-        copy.wait_send()
     for copy in plane + own:
         copy.wait()
 
@@ -167,9 +170,10 @@
     width = out_ref.shape[1]
     tile = min(COLUMN_TILE, width)
     greet(ctx_count, tensor_count, me_ctx, me_tp)
-    order = list(range(tensor_count - 1, -1, -1))
+    order = near_first(tensor_count)[::-1] + [0]
     plane, own = {}, {}
-    for k in order:
+
+    def send_back(k):
         plane[k] = []
         for m in range(1, ctx_count):
             span = pl.ds(m * cap, cap)
@@ -187,8 +191,14 @@
             slots_ref.at[k, span], returned.at[k, span], own_sem.at[k]
         )
         own[k].start()
+
+    send_back(order[0])
     along = []
-    for k in order:
+    for turn, k in enumerate(order):
+        for copy in plane[k]:
+            copy.wait_send()
+        if turn + 1 < tensor_count:
+            send_back(order[turn + 1])
         for copy in plane[k]:
             copy.wait_recv()
         own[k].wait()
@@ -221,9 +231,6 @@
         out_ref[:, columns] = total
     for copy in along:
         copy.wait_send()
-    for k in order:
-        for copy in plane[k]:
-            copy.wait_send()
 
 
 def semaphores(ctx_count, tensor_count):
@@ -354,15 +361,18 @@
     def blocked(rows):
         return rows.reshape(tensor_count, slots, model_width)
 
-    hidden = residual.astype(jnp.float32) + tensor_rows(
-        jnp.dot(attention, w_out, preferred_element_type=jnp.float32)
-    )
+    attended = tensor_rows(jnp.dot(attention, w_out, preferred_element_type=jnp.float32))
+    grad_partial = jnp.dot(d_projected, w_qkv, preferred_element_type=jnp.float32).astype(
+        jnp.bfloat16
+    )
+    attended, select, slot_gate, select_back, gated_back, grad_partial = lax.optimization_barrier(
+        (attended, select, slot_gate, select_back, gated_back, grad_partial)
+    )
+    hidden = residual.astype(jnp.float32) + attended
     inv_one = rms_inverse(hidden)
     moe_input = (hidden * inv_one * norm_moe).astype(jnp.bfloat16)
-    moe_input, d_projected = lax.optimization_barrier((moe_input, d_projected))
-    grad_attn_in = tensor_rows(
-        jnp.dot(d_projected, w_qkv, preferred_element_type=jnp.float32)
-    )
+    moe_input, grad_partial = lax.optimization_barrier((moe_input, grad_partial))
+    grad_attn_in = tensor_rows(grad_partial)
     arrived = flat(dispatch(moe_input, select, jnp.ones_like(slot_gate), cap))
     pre_gate, pre_up, active = expert_inner(arrived, gate_mat, up_mat)
     half_out = jnp.dot(active, down_mat, preferred_element_type=jnp.float32).astype(jnp.bfloat16)

time: 612 us -> 578 us (0.944)
  waiting for transfers between devices: 117 us -> 96.3 us
  Pallas kernels: 371 us -> 351 us
    pallas_call x2, Pallas kernels: 185 us -> 149 us  [combine(): pl.pallas_call(functools.partial(combine_kernel, ctx_count, tensor_count,...]
    reduce_scatter x2, waiting for transfers between devices: 46.7 us -> 26.8 us  [tensor_rows(): lax.psum_scatter(local_sum.astype(jnp.bfloat16), 'tp', scatter_dimension=...]
    pallas_call x2, Pallas kernels: 186 us -> 202 us  [dispatch(): pl.pallas_call(functools.partial(dispatch_kernel, ctx_count, tensor_count...]
    unnamed x105 -> x103, local copies, waits for them, and re-layouts: 15.6 us -> 15.7 us
  transfers between devices with their start and end apart: 8 -> 8, of which waited for: 4 -> 3; matrix products, arithmetic and copies ran while one was open for 10% -> 12% of each run, Pallas kernels for 31% -> 35%
where the time goes in v3:
time: 578 us; the launch traced here: 572 us
  Pallas kernels  351 us (61%)
  waiting for transfers between devices  96.3 us (17%)
  matrix products  65.7 us (11%)
  local copies, waits for them, and re-layouts  22.9 us (4%)
  between operations  14.5 us (3%)
  other arithmetic  13.3 us (2%)
  starting transfers between devices  8.31 us (1%)
    pallas_call x2, Pallas kernels, dispatch(): pl.pallas_call(functools.partial(dispatch_kernel, ctx_count, tensor_count...  202 us
    pallas_call x2, Pallas kernels, combine(): pl.pallas_call(functools.partial(combine_kernel, ctx_count, tensor_count,...  149 us
    all_gather x2, waiting for transfers between devices, group_rows(): return lax.all_gather(local_rows, 'tp', axis=0, tiled=True)  44.3 us
    reduce_scatter x2, waiting for transfers between devices, tensor_rows(): lax.psum_scatter(local_sum.astype(jnp.bfloat16), 'tp', scatter_dimension=...  26.8 us
    reduce_scatter x1, waiting for transfers between devices, local(): lax.psum_scatter(out_partial, 'ctx', scatter_dimension=1, tiled=True)  25.1 us
    unnamed x103, local copies, waits for them, and re-layouts  15.7 us
  transfers between devices with their start and end apart: 8, of which 3 were waited for; matrix products, arithmetic and copies ran while one was open for 12% of the time, Pallas kernels for 35%

profile of v3, /device:TPU:0, one launch (start us, length us, event | category | flops | bytes accessed | tf_op | source)
XLA Modules:
  0.0 572.2 jit_solution(3224604547970055561)
XLA Ops:
  7.2 4.5 convolution_convert_fusion.2
  12.4 4.1 collective-permute-start.1
  20.4 4.3 convolution_convert_fusion.1
  27.2 2.3 copy.34
  31.7 26.8 %reduce-scatter.4.cloned.1.call-done = bf16[128,2048]{1,0:T(8,128)(2,1)} async-done(((bf16[512,2048]{1,0:T(8,128)(2,1)}), bf16[128,2048]{1,0:T(8,128)(2,1)}) %reduce-scatter.4.cloned.1.call-update) | async-done | bytes 524304 | tf_op jit(solution)/shard_map/reduce_scatter | solution.py:55
  65.4 100.2 %shard_map.188 = bf16[4,384,2048]{2,1,0:T(8,128)(2,1)S(1)} custom-call(bf16[128,2048]{1,0:T(8,128)(2,1)S(1)} %copy-done.7, bf16[4,384,128]{2,1,0:T(8,128)(2,1)S(1)} %copy.35.select_ref, f32[4,384,1]{2,1,0:T(8,128)S(1)} %broadcast_in_dim.61.scale_ref), custom_call_target="tpu_custom_call" | custom-call | flops 805306368 | bytes 201326592 | tf_op jit(solution)/shard_map/pallas_call | solution.py:259
  165.7 3.4 fusion.12
  169.2 5.0 multiply_convert_fusion.2
  175.2 5.3 convolution_convert_fusion
  181.7 3.2 copy-done.4
  185.9 75.0 %shard_map.189 = f32[128,2048]{1,0:T(8,128)S(1)} custom-call(bf16[4,384,2048]{2,1,0:T(8,128)(2,1)S(1)} %bitcast.74, bf16[4,128,384]{2,1,0:T(8,128)(2,1)S(1)} %copy-done.9), custom_call_target="tpu_custom_call" | custom-call | flops 805306368 | bytes 201326592 | tf_op jit(solution)/shard_map/pallas_call | solution.py:281
  268.8 101.9 %shard_map.190 = bf16[4,384,2048]{2,1,0:T(8,128)(2,1)S(1)} custom-call(bf16[128,2048]{1,0:T(8,128)(2,1)S(1)} %copy-done.8, bf16[4,384,128]{2,1,0:T(8,128)(2,1)S(1)} %copy.35.select_ref, f32[4,384,1]{2,1,0:T(8,128)S(1)} %copy-done.6), custom_call_target="tpu_custom_call" | custom-call | flops 805306368 | bytes 201326592 | tf_op jit(solution)/shard_map/pallas_call | solution.py:259
  370.8 4.2 multiply_convert_fusion
  375.1 3.5 fusion.10
  378.6 5.5 add_convert_fusion
  384.1 2.8 copy-done.1
  386.9 74.0 %shard_map.191 = f32[128,2048]{1,0:T(8,128)S(1)} custom-call(bf16[4,384,2048]{2,1,0:T(8,128)(2,1)S(1)} %bitcast.65, bf16[4,128,384]{2,1,0:T(8,128)(2,1)S(1)} %bitcast.75), custom_call_target="tpu_custom_call" | custom-call | flops 805306368 | bytes 201326592 | tf_op jit(solution)/shard_map/pallas_call | solution.py:281
  464.2 44.3 %all-gather.5.cloned.1.call-done = bf16[512,2048]{1,0:T(8,128)(2,1)} async-done(((bf16[128,2048]{1,0:T(8,128)(2,1)}), bf16[512,2048]{1,0:T(8,128)(2,1)}) %all-gather.5.cloned.1.call-update) | async-done | bytes 2097168 | tf_op jit(solution)/shard_map/all_gather | solution.py:61
  508.5 4.9 convolution_bitcast_fusion
  513.4 7.1 %fusion.2 = bf16[1,384,2048]{2,1,0:T(8,128)(2,1)} fusion(bf16[1536,384]{1,0:T(8,128)(2,1)} %copy-done.45, bf16[1536,2048]{1,0:T(8,128)(2,1)} %bitcast.73), kind=kOutput, calls=%fused_computation.10 | convolution fusion | flops 2416705536 | bytes 9043968 | tf_op jit(solution)/shard_map/sf,sd->fd/dot_general | solution.py:50
  520.5 8.2 %fusion.1 = bf16[1,2048,384]{2,1,0:T(8,128)(2,1)} fusion(bf16[1536,2048]{1,0:T(8,128)(2,1)} %bitcast.68, bf16[1536,384]{1,0:T(8,128)(2,1)S(1)} %copy-done.30), kind=kOutput, calls=%fused_computation.9 | convolution fusion | flops 2416705536 | bytes 9043968 | tf_op jit(solution)/shard_map/sd,sf->df/dot_general | solution.py:49
  528.8 4.7 fusion
  533.5 2.8 convolution_convert_fusion.6
  538.5 25.1 %reduce-scatter.8.cloned.1.call-done = f32[512,256]{0,1:T(8,128)} async-done(((f32[512,2048]{0,1:T(8,128)}), f32[512,256]{0,1:T(8,128)}) %reduce-scatter.8.cloned.1.call-update) | async-done | bytes 524304 | tf_op jit(solution)/shard_map/reduce_scatter | solution.py:405
  (154 shorter events, 34.6 us)
Async XLA Ops:
  7.2 13.2 %copy-start = (bf16[768,2048]{1,0:T(8,128)(2,1)S(1)}, bf16[768,2048]{1,0:T(8,128)(2,1)}, u32[]{:S(2)}) copy-start(bf16[768,2048]{1,0:T(8,128)(2,1)} %param.16) | copy-start | bytes 9437188
  7.2 51.3 %reduce-scatter.4.cloned.1.call-start = ((), (), s32[]{:S(2)}) async-start(), calls=%async_computation.3 | async-start | bytes 2621440 | tf_op jit(solution)/shard_map/reduce_scatter | solution.py:55
  11.8 168.8 %reduce-scatter.6.cloned.1.call-start = ((), (), s32[]{:S(2)}) async-start(), calls=%async_computation.4 | async-start | bytes 2621440 | tf_op jit(solution)/shard_map/reduce_scatter | solution.py:55
  12.4 12.4 %collective-permute-start.1 = (f32[128,8]{0,1:T(8,128)S(1)}, f32[128,8]{0,1:T(8,128)S(1)}, u32[]{:S(2)}, u32[]{:S(2)}) collective-permute-start(f32[128,8]{0,1:T(8,128)S(1)} %get-tuple-element.67), channel_id=1, source_target_pairs={{0,2},{1,3},{2,0},{3,1},{4,6},{5,7},{6,4},{7,5},{8,10},{9,11},{10,... | collective-permute-start | bytes 12296 | tf_op jit(solution)/shard_map/ppermute | solution.py:332
  16.5 8.2 %collective-permute-start = (f32[128,8]{0,1:T(8,128)S(1)}, f32[128,8]{0,1:T(8,128)S(1)}, u32[]{:S(2)}, u32[]{:S(2)}) collective-permute-start(f32[128,8]{0,1:T(8,128)S(1)} %get-tuple-element.67), channel_id=1, source_target_pairs={{0,1},{1,2},{2,3},{3,0},{4,5},{5,6},{6,7},{7,4},{8,9},{9,10},{10,1... | collective-permute-start | bytes 12296 | tf_op jit(solution)/shard_map/ppermute | solution.py:332
  18.1 6.7 %collective-permute-start.2 = (f32[128,8]{0,1:T(8,128)S(1)}, f32[128,8]{0,1:T(8,128)S(1)}, u32[]{:S(2)}, u32[]{:S(2)}) collective-permute-start(f32[128,8]{0,1:T(8,128)S(1)} %get-tuple-element.67), channel_id=1, source_target_pairs={{0,3},{1,0},{2,1},{3,2},{4,7},{5,4},{6,5},{7,6},{8,11},{9,8},{10,9... | collective-permute-start | bytes 12296 | tf_op jit(solution)/shard_map/ppermute | solution.py:332
  29.5 32.4 %copy-start.31 = (f32[2048]{0:T(1024)S(1)}, f32[2048]{0:T(1024)}, u32[]{:S(2)}) copy-start(f32[2048]{0:T(1024)} %param.17) | copy-start | bytes 24580
  62.9 321.2 %all-gather.3.cloned.1.call-start = ((), (), s32[]{:S(2)}) async-start(), calls=%async_computation.5 | async-start | bytes 2621440 | tf_op jit(solution)/shard_map/all_gather | solution.py:61
  65.4 100.2 %copy-start.23 = (bf16[1,2048,384]{2,1,0:T(8,128)(2,1)S(1)}, bf16[1,2048,384]{2,1,0:T(8,128)(2,1)}, u32[]{:S(2)}) copy-start(bf16[1,2048,384]{2,1,0:T(8,128)(2,1)} %param.21) | copy-start | bytes 4718596
  181.7 80.7 %copy-start.15 = (f32[128,2048]{1,0:T(8,128)}, f32[128,2048]{1,0:T(8,128)S(1)}, u32[]{:S(2)}) copy-start(f32[128,2048]{1,0:T(8,128)S(1)} %convert_element_type.106) | copy-start | bytes 3145732
  185.9 75.0 %copy-start.11 = (f32[128,2048]{1,0:T(8,128)S(1)}, f32[128,2048]{1,0:T(8,128)}, u32[]{:S(2)}) copy-start(f32[128,2048]{1,0:T(8,128)} %copy-done.10) | copy-start | bytes 3145732
  185.9 75.0 %copy-start.18 = (bf16[128,2048]{1,0:T(8,128)(2,1)S(1)}, bf16[128,2048]{1,0:T(8,128)(2,1)}, u32[]{:S(2)}) copy-start(bf16[128,2048]{1,0:T(8,128)(2,1)} %param.14) | copy-start | bytes 1572868
  264.7 243.8 %all-gather.5.cloned.1.call-start = ((), (), s32[]{:S(2)}) async-start(), calls=%async_computation.6 | async-start | bytes 2621440 | tf_op jit(solution)/shard_map/all_gather | solution.py:61
  268.8 101.9 %copy-start.44 = (bf16[1,384,2048]{2,1,0:T(8,128)(2,1)S(1)}, bf16[1,384,2048]{2,1,0:T(8,128)(2,1)}, u32[]{:S(2)}) copy-start(bf16[1,384,2048]{2,1,0:T(8,128)(2,1)} %param.23) | copy-start | bytes 4718596
  268.8 101.9 %copy-start.47 = (f32[1536,384]{1,0:T(8,128)S(1)}, f32[1536,384]{1,0:T(8,128)}, u32[]{:S(2)}) copy-start(f32[1536,384]{1,0:T(8,128)} %copy-done.46) | copy-start | bytes 7077892
  268.8 101.9 %copy-start.48 = (f32[1536,384]{1,0:T(8,128)S(1)}, f32[1536,384]{1,0:T(8,128)}, u32[]{:S(2)}) copy-start(f32[1536,384]{1,0:T(8,128)} %get-tuple-element.69) | copy-start | bytes 7077892
  386.9 74.0 %copy-start.12 = (f32[128,2048]{1,0:T(8,128)S(1)}, f32[128,2048]{1,0:T(8,128)}, u32[]{:S(2)}) copy-start(f32[128,2048]{1,0:T(8,128)} %copy-done.10) | copy-start | bytes 3145732
  386.9 74.0 %copy-start.19 = (bf16[128,2048]{1,0:T(8,128)(2,1)S(1)}, bf16[128,2048]{1,0:T(8,128)(2,1)}, u32[]{:S(2)}) copy-start(bf16[128,2048]{1,0:T(8,128)(2,1)} %param.14) | copy-start | bytes 1572868
  386.9 74.0 %copy-start.34 = (f32[128]{0:T(128)S(1)}, f32[128]{0:T(128)}, u32[]{:S(2)}) copy-start(f32[128]{0:T(128)} %copy-done.33) | copy-start | bytes 1540
  464.1 99.5 %reduce-scatter.8.cloned.1.call-start = ((), (), s32[]{:S(2)}) async-start(), calls=%async_computation.7 | async-start | bytes 4718592 | tf_op jit(solution)/shard_map/reduce_scatter | solution.py:405
  513.4 7.1 %copy-start.30 = (bf16[1536,384]{1,0:T(8,128)(2,1)S(1)}, bf16[1536,384]{1,0:T(8,128)(2,1)}, u32[]{:S(2)}) copy-start(bf16[1536,384]{1,0:T(8,128)(2,1)} %copy-done.29) | copy-start | bytes 3538948
  513.4 15.3 %slice-start = ((s8[6291456]{0:T(1024)(128)(4,1)}), s8[4194304]{0:T(1024)(128)(4,1)S(1)}, s32[]{:S(2)}) async-start(s8[6291456]{0:T(1024)(128)(4,1)} %bitcast.69), calls=%async_computation.8 | async-start | bytes 8388608
  520.5 8.2 %slice-start.1 = ((s8[6291456]{0:T(1024)(128)(4,1)}), s8[2097152]{0:T(1024)(128)(4,1)S(1)}, s32[]{:S(2)}) async-start(s8[6291456]{0:T(1024)(128)(4,1)} %bitcast.69), calls=%async_computation.9 | async-start | bytes 4194304
  520.5 8.2 %copy-start.28 = (bf16[1536,384]{1,0:T(8,128)(2,1)S(1)}, bf16[1536,384]{1,0:T(8,128)(2,1)}, u32[]{:S(2)}) copy-start(bf16[1536,384]{1,0:T(8,128)(2,1)} %copy-done.27) | copy-start | bytes 3538948
  (35 other events, 88.4 us)
Sparse Core Ops, SparseCore 0:
  11.9 46.5 reduce-scatter.3
  63.0 63.1 reduce-scatter.5
  264.9 62.3 all-gather.2
  464.2 44.2 all-gather.4
  513.5 50.0 reduce-scatter.7

commit v4 on v3

--- a/solution.py
+++ b/solution.py
@@ -371,28 +371,29 @@
     hidden = residual.astype(jnp.float32) + attended
     inv_one = rms_inverse(hidden)
     moe_input = (hidden * inv_one * norm_moe).astype(jnp.bfloat16)
-    moe_input, grad_partial = lax.optimization_barrier((moe_input, grad_partial))
+    arrived = flat(dispatch(moe_input, select, jnp.ones_like(slot_gate), cap))
+    arrived, grad_partial = lax.optimization_barrier((arrived, grad_partial))
     grad_attn_in = tensor_rows(grad_partial)
-    arrived = flat(dispatch(moe_input, select, jnp.ones_like(slot_gate), cap))
     pre_gate, pre_up, active = expert_inner(arrived, gate_mat, up_mat)
     half_out = jnp.dot(active, down_mat, preferred_element_type=jnp.float32).astype(jnp.bfloat16)
-    half_out, grad_attn_in = lax.optimization_barrier((half_out, grad_attn_in))
     stream_sum = hidden + combine(blocked(half_out), gated_back, cap)
     stream = stream_sum.astype(jnp.bfloat16)
     inv_two = rms_inverse(stream_sum)
     grad_stream = d_stream.astype(jnp.float32) + rms_grad(
         stream_sum, norm_attn, inv_two, grad_attn_in
     )
-    attn_rows = group_rows((stream_sum * inv_two * norm_attn).astype(jnp.bfloat16))
+    attn_input = (stream_sum * inv_two * norm_attn).astype(jnp.bfloat16)
     grad_arrived = flat(dispatch(grad_stream.astype(jnp.bfloat16), select, slot_gate, cap))
+    grad_arrived, attn_input = lax.optimization_barrier((grad_arrived, attn_input))
+    attn_rows = group_rows(attn_input)
     input_part, gate_grad, up_grad, down_grad = half_backward(
         arrived, grad_arrived, pre_gate, pre_up, active, gate_mat, up_mat, down_mat
     )
-    input_part, attn_rows = lax.optimization_barrier((input_part, attn_rows))
+    grad_moe_in = combine(blocked(input_part), select_back, cap)
+    grad_moe_in, attn_rows = lax.optimization_barrier((grad_moe_in, attn_rows))
     projected = jnp.einsum(
         "td,od->to", attn_rows, w_qkv, preferred_element_type=jnp.float32
     ).astype(jnp.bfloat16)
-    grad_moe_in = combine(blocked(input_part), select_back, cap)
     grad_hidden = grad_stream + rms_grad(hidden, norm_moe, inv_one, grad_moe_in)
     grad_residual = grad_hidden.astype(jnp.bfloat16)
     grad_rows_all = group_rows(grad_residual)

time: 578 us -> 533 us (0.922)
  Pallas kernels: 351 us -> 292 us
  matrix products: 65.7 us -> 79.2 us
  local copies, waits for them, and re-layouts: 22.9 us -> 15.2 us
  other arithmetic: 13.3 us -> 20 us
    pallas_call x2, Pallas kernels: 202 us -> 141 us  [dispatch(): pl.pallas_call(functools.partial(dispatch_kernel, ctx_count, tensor_count...]
    unnamed x103 -> x75, local copies, waits for them, and re-layouts: 15.7 us -> 9.24 us
  transfers between devices with their start and end apart: 8 -> 8, of which waited for: 3 -> 3; matrix products, arithmetic and copies ran while one was open for 12% -> 15% of each run, Pallas kernels for 35% -> 29%
where the time goes in v4:
time: 533 us; the launch traced here: 527 us
  Pallas kernels  292 us (55%)
  waiting for transfers between devices  96.3 us (18%)
  matrix products  79.2 us (15%)
  other arithmetic  20 us (4%)
  local copies, waits for them, and re-layouts  15.2 us (3%)
  between operations  14.7 us (3%)
  starting transfers between devices  8.77 us (2%)
    pallas_call x2, Pallas kernels, combine(): pl.pallas_call(functools.partial(combine_kernel, ctx_count, tensor_count,...  151 us
    pallas_call x2, Pallas kernels, dispatch(): pl.pallas_call(functools.partial(dispatch_kernel, ctx_count, tensor_count...  141 us
    all_gather x2, waiting for transfers between devices, group_rows(): return lax.all_gather(local_rows, 'tp', axis=0, tiled=True)  43.6 us
    reduce_scatter x2, waiting for transfers between devices, tensor_rows(): lax.psum_scatter(local_sum.astype(jnp.bfloat16), 'tp', scatter_dimension=...  27.4 us
    reduce_scatter x1, waiting for transfers between devices, local(): lax.psum_scatter(out_partial, 'ctx', scatter_dimension=1, tiled=True)  25.3 us
  transfers between devices with their start and end apart: 8, of which 3 were waited for; matrix products, arithmetic and copies ran while one was open for 15% of the time, Pallas kernels for 29%

profile of v4, /device:TPU:0, one launch (start us, length us, event | category | flops | bytes accessed | tf_op | source)
XLA Modules:
  0.0 526.7 jit_solution(4854522105081093075)
XLA Ops:
  7.2 4.5 convolution_convert_fusion.2
  12.4 4.1 collective-permute-start.1
  20.4 4.3 convolution_convert_fusion.1
  31.1 27.4 %reduce-scatter.4.cloned.1.call-done = bf16[128,2048]{1,0:T(8,128)(2,1)} async-done(((bf16[512,2048]{1,0:T(8,128)(2,1)}), bf16[128,2048]{1,0:T(8,128)(2,1)}) %reduce-scatter.4.cloned.1.call-update) | async-done | bytes 524304 | tf_op jit(solution)/shard_map/reduce_scatter | solution.py:55
  64.7 71.8 %shard_map.188 = bf16[4,384,2048]{2,1,0:T(8,128)(2,1)S(1)} custom-call(bf16[128,2048]{1,0:T(8,128)(2,1)S(1)} %multiply_convert_fusion.4.rows_ref, bf16[4,384,128]{2,1,0:T(8,128)(2,1)S(1)} %copy.35.select_ref, f32[4,384,1]{2,1,0:T(8,128)S(1)} %broadcast_in_dim.61.scale_ref), custom_call_target="tpu_custom_call" | custom-call | flops 805306368 | bytes 201326592 | tf_op jit(solution)/shard_map/pallas_call | solution.py:259
  140.5 6.1 %fusion.12 = f32[1536,384]{1,0:T(8,128)S(1)} fusion(bf16[1536,2048]{1,0:T(8,128)(2,1)} %bitcast.66, bf16[1,2048,384]{2,1,0:T(8,128)(2,1)} %param.21), kind=kOutput, calls=%fused_computation.24 | convolution fusion | flops 2415919104 | bytes 10223616 | tf_op jit(solution)/shard_map/dot_general | solution.py:30
  146.6 8.8 %multiply_convert_fusion.2 = (bf16[1536,384]{1,0:T(8,128)(2,1)S(1)}, f32[1536,384]{1,0:T(8,128)}) fusion(f32[1536,384]{1,0:T(8,128)S(1)} %fusion.12, bf16[1536,2048]{1,0:T(8,128)(2,1)} %bitcast.67, bf16[1,2048,384]{2,1,0:T(8,128)(2,1)S(1)} %copy-done.16), kind=kOutput, calls=%fused_computation.13 | convolution fusion | flops 2419458048 | bytes 13762560 | tf_op jit(solution)/shard_map/dot_general | solution.py:31
  155.4 3.7 convolution_convert_fusion
  159.1 74.9 %shard_map.189 = f32[128,2048]{1,0:T(8,128)S(1)} custom-call(bf16[4,384,2048]{2,1,0:T(8,128)(2,1)S(1)} %bitcast.74, bf16[4,128,384]{2,1,0:T(8,128)(2,1)S(1)} %copy-done.7), custom_call_target="tpu_custom_call" | custom-call | flops 805306368 | bytes 201326592 | tf_op jit(solution)/shard_map/pallas_call | solution.py:281
  238.6 2.7 multiply_convert_fusion.3
  241.4 69.7 %shard_map.190 = bf16[4,384,2048]{2,1,0:T(8,128)(2,1)S(1)} custom-call(bf16[128,2048]{1,0:T(8,128)(2,1)S(1)} %get-tuple-element.63.rows_ref, bf16[4,384,128]{2,1,0:T(8,128)(2,1)S(1)} %copy.35.select_ref, f32[4,384,1]{2,1,0:T(8,128)S(1)} %copy-done.6), custom_call_target="tpu_custom_call" | custom-call | flops 805306368 | bytes 201326592 | tf_op jit(solution)/shard_map/pallas_call | solution.py:259
  311.1 2.6 copy-done.4
  314.0 8.9 %multiply_convert_fusion = (bf16[1536,384]{1,0:T(8,128)(2,1)S(1)}, bf16[1536,384]{1,0:T(8,128)(2,1)S(1)}) fusion(f32[1536,384]{1,0:T(8,128)} %copy-done.34, f32[1536,384]{1,0:T(8,128)} %get-tuple-element.69, bf16[1536,2048]{1,0:T(8,128)(2,1)} %bitcast.72, bf16[1,384,2048]{2,1,0:T(8,128)(2,1)} %param.23), kind=kOutput, calls=%fused_computation.11 | convolution fusion | flops 2423586816 | bytes 14942208 | tf_op jit(solution)/shard_map/sd,fd->sf/dot_general | solution.py:39
  323.0 6.4 %fusion.10 = f32[1536,2048]{1,0:T(8,128)} fusion(bf16[1536,384]{1,0:T(8,128)(2,1)S(1)} %get-tuple-element.61, bf16[1,2048,384]{2,1,0:T(8,128)(2,1)S(1)} %copy-done.15), kind=kOutput, calls=%fused_computation.22 | convolution fusion | flops 2415919104 | bytes 15335424 | tf_op jit(solution)/shard_map/sf,df->sd/dot_general | solution.py:44
  329.5 6.7 %add_convert_fusion = bf16[1536,2048]{1,0:T(8,128)(2,1)S(1)} fusion(f32[1536,2048]{1,0:T(8,128)} %fusion.10, bf16[1536,384]{1,0:T(8,128)(2,1)S(1)} %get-tuple-element.60, bf16[1,2048,384]{2,1,0:T(8,128)(2,1)S(1)} %copy-done.17), kind=kOutput, calls=%fused_computation | convolution fusion | flops 2422210560 | bytes 21626880 | tf_op jit(solution)/shard_map/sf,df->sd/dot_general | solution.py:46
  336.2 76.1 %shard_map.191 = f32[128,2048]{1,0:T(8,128)S(1)} custom-call(bf16[4,384,2048]{2,1,0:T(8,128)(2,1)S(1)} %bitcast.65, bf16[4,128,384]{2,1,0:T(8,128)(2,1)S(1)} %bitcast.75), custom_call_target="tpu_custom_call" | custom-call | flops 805306368 | bytes 201326592 | tf_op jit(solution)/shard_map/pallas_call | solution.py:281
  415.7 3.0 add_convert_fusion.1
  419.0 43.6 %all-gather.5.cloned.1.call-done = bf16[512,2048]{1,0:T(8,128)(2,1)} async-done(((bf16[128,2048]{1,0:T(8,128)(2,1)}), bf16[512,2048]{1,0:T(8,128)(2,1)}) %all-gather.5.cloned.1.call-update) | async-done | bytes 2097168 | tf_op jit(solution)/shard_map/all_gather | solution.py:61
  462.6 4.9 convolution_bitcast_fusion
  467.6 7.1 %fusion.2 = bf16[1,384,2048]{2,1,0:T(8,128)(2,1)} fusion(bf16[1536,384]{1,0:T(8,128)(2,1)} %copy-done.33, bf16[1536,2048]{1,0:T(8,128)(2,1)} %bitcast.73), kind=kOutput, calls=%fused_computation.10 | convolution fusion | flops 2416705536 | bytes 9043968 | tf_op jit(solution)/shard_map/sf,sd->fd/dot_general | solution.py:50
  474.7 8.2 %fusion.1 = bf16[1,2048,384]{2,1,0:T(8,128)(2,1)} fusion(bf16[1536,2048]{1,0:T(8,128)(2,1)} %bitcast.68, bf16[1536,384]{1,0:T(8,128)(2,1)S(1)} %copy-done.21), kind=kOutput, calls=%fused_computation.9 | convolution fusion | flops 2416705536 | bytes 9043968 | tf_op jit(solution)/shard_map/sd,sf->df/dot_general | solution.py:49
  482.9 4.6 fusion
  487.5 2.8 convolution_convert_fusion.6
  492.5 25.3 %reduce-scatter.8.cloned.1.call-done = f32[512,256]{0,1:T(8,128)} async-done(((f32[512,2048]{0,1:T(8,128)}), f32[512,256]{0,1:T(8,128)}) %reduce-scatter.8.cloned.1.call-update) | async-done | bytes 524304 | tf_op jit(solution)/shard_map/reduce_scatter | solution.py:406
  (125 shorter events, 33.8 us)
Async XLA Ops:
  7.2 13.2 %copy-start = (bf16[768,2048]{1,0:T(8,128)(2,1)S(1)}, bf16[768,2048]{1,0:T(8,128)(2,1)}, u32[]{:S(2)}) copy-start(bf16[768,2048]{1,0:T(8,128)(2,1)} %param.16) | copy-start | bytes 9437188
  7.2 51.3 %reduce-scatter.4.cloned.1.call-start = ((), (), s32[]{:S(2)}) async-start(), calls=%async_computation.3 | async-start | bytes 2621440 | tf_op jit(solution)/shard_map/reduce_scatter | solution.py:55
  11.8 225.1 %reduce-scatter.6.cloned.1.call-start = ((), (), s32[]{:S(2)}) async-start(), calls=%async_computation.4 | async-start | bytes 2621440 | tf_op jit(solution)/shard_map/reduce_scatter | solution.py:55
  12.4 12.4 %collective-permute-start.1 = (f32[128,8]{0,1:T(8,128)S(1)}, f32[128,8]{0,1:T(8,128)S(1)}, u32[]{:S(2)}, u32[]{:S(2)}) collective-permute-start(f32[128,8]{0,1:T(8,128)S(1)} %get-tuple-element.67), channel_id=1, source_target_pairs={{0,2},{1,3},{2,0},{3,1},{4,6},{5,7},{6,4},{7,5},{8,10},{9,11},{10,... | collective-permute-start | bytes 12296 | tf_op jit(solution)/shard_map/ppermute | solution.py:332
  16.6 8.3 %collective-permute-start = (f32[128,8]{0,1:T(8,128)S(1)}, f32[128,8]{0,1:T(8,128)S(1)}, u32[]{:S(2)}, u32[]{:S(2)}) collective-permute-start(f32[128,8]{0,1:T(8,128)S(1)} %get-tuple-element.67), channel_id=1, source_target_pairs={{0,1},{1,2},{2,3},{3,0},{4,5},{5,6},{6,7},{7,4},{8,9},{9,10},{10,1... | collective-permute-start | bytes 12296 | tf_op jit(solution)/shard_map/ppermute | solution.py:332
  18.1 6.7 %collective-permute-start.2 = (f32[128,8]{0,1:T(8,128)S(1)}, f32[128,8]{0,1:T(8,128)S(1)}, u32[]{:S(2)}, u32[]{:S(2)}) collective-permute-start(f32[128,8]{0,1:T(8,128)S(1)} %get-tuple-element.67), channel_id=1, source_target_pairs={{0,3},{1,0},{2,1},{3,2},{4,7},{5,4},{6,5},{7,6},{8,11},{9,8},{10,9... | collective-permute-start | bytes 12296 | tf_op jit(solution)/shard_map/ppermute | solution.py:332
  31.1 31.9 %copy-start.22 = (f32[2048]{0:T(1024)S(1)}, f32[2048]{0:T(1024)}, u32[]{:S(2)}) copy-start(f32[2048]{0:T(1024)} %param.17) | copy-start | bytes 24580
  139.1 274.2 %all-gather.3.cloned.1.call-start = ((), (), s32[]{:S(2)}) async-start(), calls=%async_computation.5 | async-start | bytes 2621440 | tf_op jit(solution)/shard_map/all_gather | solution.py:61
  146.6 8.9 %copy-start.34 = (f32[1536,384]{1,0:T(8,128)}, f32[1536,384]{1,0:T(8,128)S(1)}, u32[]{:S(2)}) copy-start(f32[1536,384]{1,0:T(8,128)S(1)} %fusion.12) | copy-start | bytes 7077892
  146.6 8.8 %copy-start.32 = (bf16[1,384,2048]{2,1,0:T(8,128)(2,1)S(1)}, bf16[1,384,2048]{2,1,0:T(8,128)(2,1)}, u32[]{:S(2)}) copy-start(bf16[1,384,2048]{2,1,0:T(8,128)(2,1)} %param.23) | copy-start | bytes 4718596
  159.1 75.0 %copy-start.9 = (f32[128,2048]{1,0:T(8,128)S(1)}, f32[128,2048]{1,0:T(8,128)}, u32[]{:S(2)}) copy-start(f32[128,2048]{1,0:T(8,128)} %copy-done.8) | copy-start | bytes 3145732
  159.1 75.0 %copy-start.12 = (bf16[128,2048]{1,0:T(8,128)(2,1)S(1)}, bf16[128,2048]{1,0:T(8,128)(2,1)}, u32[]{:S(2)}) copy-start(bf16[128,2048]{1,0:T(8,128)(2,1)} %param.14) | copy-start | bytes 1572868
  238.6 72.5 %copy-start.26 = (f32[128]{0:T(128)}, f32[128]{0:T(128)S(1)}, u32[]{:S(2)}) copy-start(f32[128]{0:T(128)S(1)} %broadcast_multiply_fusion.2) | copy-start | bytes 1540
  313.8 148.9 %all-gather.5.cloned.1.call-start = ((), (), s32[]{:S(2)}) async-start(), calls=%async_computation.6 | async-start | bytes 2621440 | tf_op jit(solution)/shard_map/all_gather | solution.py:61
  314.0 9.0 %copy-start.15 = (bf16[1,2048,384]{2,1,0:T(8,128)(2,1)S(1)}, bf16[1,2048,384]{2,1,0:T(8,128)(2,1)}, u32[]{:S(2)}) copy-start(bf16[1,2048,384]{2,1,0:T(8,128)(2,1)} %param.21) | copy-start | bytes 4718596
  323.0 6.5 %copy-start.18 = (bf16[1536,384]{1,0:T(8,128)(2,1)}, bf16[1536,384]{1,0:T(8,128)(2,1)S(1)}, u32[]{:S(2)}) copy-start(bf16[1536,384]{1,0:T(8,128)(2,1)S(1)} %get-tuple-element.61) | copy-start | bytes 3538948
  323.0 6.5 %copy-start.20 = (bf16[1536,384]{1,0:T(8,128)(2,1)}, bf16[1536,384]{1,0:T(8,128)(2,1)S(1)}, u32[]{:S(2)}) copy-start(bf16[1536,384]{1,0:T(8,128)(2,1)S(1)} %get-tuple-element.60) | copy-start | bytes 3538948
  329.5 6.7 %copy-start.5 = (bf16[4,384,128]{1,2,0:T(8,128)(2,1)S(1)}, bf16[4,384,128]{1,2,0:T(8,128)(2,1)}, u32[]{:S(2)}) copy-start(bf16[4,384,128]{1,2,0:T(8,128)(2,1)} %get-tuple-element.21) | copy-start | bytes 1179652
  336.2 77.1 %copy-start.24 = (f32[128]{0:T(128)S(1)}, f32[128]{0:T(128)}, u32[]{:S(2)}) copy-start(f32[128]{0:T(128)} %add_rsqrt_fusion.1) | copy-start | bytes 1540
  418.7 99.1 %reduce-scatter.8.cloned.1.call-start = ((), (), s32[]{:S(2)}) async-start(), calls=%async_computation.7 | async-start | bytes 4718592 | tf_op jit(solution)/shard_map/reduce_scatter | solution.py:406
  467.6 7.1 %copy-start.21 = (bf16[1536,384]{1,0:T(8,128)(2,1)S(1)}, bf16[1536,384]{1,0:T(8,128)(2,1)}, u32[]{:S(2)}) copy-start(bf16[1536,384]{1,0:T(8,128)(2,1)} %copy-done.20) | copy-start | bytes 3538948
  467.6 15.3 %slice-start = ((s8[6291456]{0:T(1024)(128)(4,1)}), s8[4194304]{0:T(1024)(128)(4,1)S(1)}, s32[]{:S(2)}) async-start(s8[6291456]{0:T(1024)(128)(4,1)} %bitcast.69), calls=%async_computation.8 | async-start | bytes 8388608
  474.7 8.2 %slice-start.1 = ((s8[6291456]{0:T(1024)(128)(4,1)}), s8[2097152]{0:T(1024)(128)(4,1)S(1)}, s32[]{:S(2)}) async-start(s8[6291456]{0:T(1024)(128)(4,1)} %bitcast.69), calls=%async_computation.9 | async-start | bytes 4194304
  474.7 8.2 %copy-start.19 = (bf16[1536,384]{1,0:T(8,128)(2,1)S(1)}, bf16[1536,384]{1,0:T(8,128)(2,1)}, u32[]{:S(2)}) copy-start(bf16[1536,384]{1,0:T(8,128)(2,1)} %copy-done.18) | copy-start | bytes 3538948
  (21 other events, 59.2 us)
Sparse Core Ops, SparseCore 0:
  11.9 46.5 reduce-scatter.3
  139.2 43.6 reduce-scatter.5
  313.9 58.8 all-gather.2
  418.8 43.7 all-gather.4
  467.7 50.0 reduce-scatter.7
